TPU v7x, 32 devices: a whole 2x2x4 slice. The times are simulated.
32 devices in a mesh: dp: 8 (over y, x, core), mp: 4 (over z).
Axes of the slice: x: 2, y: 2, z: 4, core: 2. Of those that a mesh axis runs over, the one named last changes fastest.
Arguments:
- response_query: bfloat16 [384, 8, 6144], P('dp', None, 'mp'), may hold values from -80 to 80, as said below
- response_keys: bfloat16 [2, 384, 8, 768], P(None, 'dp'), may hold values from -8 to 8
- prompt_cache: bfloat16 [2, 8, 1024, 768], P(None, 'dp'), may hold values from -6 to 6
- lengths: int32 [384], P('dp'), may hold values from 1 to 8, as said below
- owners: int32 [384], P('dp'), may hold values from 0 to 7, as said below
- pairing: int32 [384], replicated, may hold values from 0 to 383, each once
- residual: bfloat16 [384, 8192], P(None, 'dp'), may hold values from -90 to 90
- output_weight: bfloat16 [6144, 8192], P('mp', 'dp'), may hold values from -0.3125 to 0.3125
- norm_gain: float32 [8192], P('dp'), may hold values from 0.1 to 1.9
- reward_head: float32 [8192], P('dp'), may hold values from -0.0625 to 0.0625
Outputs:
- attention_rows: bfloat16 [384, 8, 6144], P('dp', None, 'mp')
- rewards: float32 [384], replicated
- pair_loss: float32 [], replicated
- weight_gradient: float32 [6144, 8192], P('mp', 'dp')
- head_gradient: float32 [8192], P('dp')
- pooled_gradient: float32 [384, 6144], P('dp', 'mp')
Inputs may be any that keep to these rules, and one draw needn't show every extreme that they name: `response_query`: drawn jointly with response_keys. `lengths`: every dp index holds a response of length 8. The responses of one dp index spread over owners as evenly as possible: each owner receives at most 6 of them, and some owner receives exactly 6.
All inputs are finite; a program needn't handle non-finite values.
Results may differ from a plain program's by a relative error of at most 0.0056.
Values may be sent and summed in bfloat16 or wider, within the bound.
A program may use at most 64 MiB of HBM per device.

v0:
```python
import math

import jax
import jax.numpy as jnp
from jax import lax
from jax.sharding import PartitionSpec as P

D = 8192
HD = 128
Q_HEADS = 48
KV_HEADS = 6


EPSILON = 1e-05


def bradley_terry(rewards, pairing):
    chosen = pairing[0::2]
    rejected = pairing[1::2]
    margin = rewards[chosen] - rewards[rejected]
    loss_value = jnp.mean(jax.nn.softplus(-margin))
    slope = -jax.nn.sigmoid(-margin) / margin.shape[0]
    reward_slope = jnp.zeros_like(rewards).at[chosen].add(slope).at[rejected].add(-slope)
    return (loss_value, reward_slope)


def shards(
    response_query,
    response_keys,
    prompt_cache,
    lengths,
    owners,
    pairing,
    residual,
    output_weight,
    norm_gain,
    reward_head,
):
    groups = lax.axis_size("dp")
    model_rank = lax.axis_index("mp")
    held_count = response_query.shape[0]
    slot_count = response_query.shape[1]
    head_width = response_query.shape[2]
    local_heads = head_width // HD
    group_size = Q_HEADS // KV_HEADS
    per_owner = (held_count + groups - 1) // groups
    if group_size % local_heads == 0:
        window = 1
    elif local_heads % group_size == 0:
        window = local_heads // group_size
    else:
        window = min(KV_HEADS, (local_heads - 1) // group_size + 2)
    first_head = jnp.minimum(model_rank * local_heads // group_size, KV_HEADS - window)
    head_slot = (model_rank * local_heads + jnp.arange(local_heads)) // group_size - first_head
    score_scale = 1.0 / math.sqrt(HD)
    own_window = lax.dynamic_slice_in_dim(response_keys, first_head * HD, window * HD, 3)
    spread = own_window.reshape(2, held_count, slot_count, window, HD)
    picked = jnp.take(spread, head_slot, axis=3).reshape(
        2, held_count, slot_count, local_heads * HD
    )
    key_pick = jnp.arange(local_heads)
    outgoing_keys = jnp.concatenate([picked[0], picked[1]], axis=-1)
    positions = jnp.arange(held_count)
    earlier = (owners[None, :] == owners[:, None]) & (positions[None, :] < positions[:, None])
    target = owners * per_owner + jnp.sum(earlier, axis=1)
    capacity = groups * per_owner
    query_buffer = (
        jnp.zeros((capacity, slot_count, head_width), jnp.bfloat16).at[target].set(response_query)
    )
    query_buffer = query_buffer.reshape(groups, per_owner, slot_count, head_width)
    key_buffer = (
        jnp.zeros((capacity, slot_count, 2 * local_heads * HD), jnp.bfloat16)
        .at[target]
        .set(outgoing_keys)
    )
    key_buffer = key_buffer.reshape(groups, per_owner, slot_count, 2 * local_heads * HD)
    length_buffer = (
        jnp.zeros((capacity,), jnp.int32).at[target].set(lengths).reshape(groups, per_owner)
    )
    prefix = lax.dynamic_slice_in_dim(prompt_cache[:, 0], first_head * HD, window * HD, 2)
    query_in = lax.all_to_all(query_buffer, "dp", split_axis=0, concat_axis=0, tiled=True)
    keys_in = lax.all_to_all(key_buffer, "dp", split_axis=0, concat_axis=0, tiled=True)
    length_in = lax.all_to_all(length_buffer, "dp", split_axis=0, concat_axis=0, tiled=True)
    sources = query_in.shape[0]
    item_count = query_in.shape[1]
    blocks = sources * item_count
    row_count = blocks * slot_count
    queries = query_in.reshape(blocks, slot_count, local_heads, HD)
    own_keys = keys_in.reshape(blocks, slot_count, 2, local_heads, HD)
    live_length = length_in.reshape(blocks)
    offsets = jnp.arange(slot_count)
    allowed = (offsets[None, None, :] <= offsets[None, :, None]) & (
        offsets[None, None, :] < live_length[:, None, None]
    )
    valid_rows = offsets[None, :] < live_length[:, None]

    def one_head(head_index):
        query_head = lax.dynamic_index_in_dim(queries, head_index, 2, keepdims=False)
        self_pair = lax.dynamic_index_in_dim(own_keys, key_pick[head_index], 3, keepdims=False)
        cache_pair = lax.dynamic_slice_in_dim(prefix, head_slot[head_index] * HD, HD, 2)
        flat_query = query_head.reshape(row_count, HD)
        far_scores = (
            lax.dot_general(
                flat_query,
                cache_pair[0],
                (((1,), (1,)), ((), ())),
                preferred_element_type=jnp.float32,
            )
            * score_scale
        )
        near_scores = (
            jnp.einsum(
                "bth,bsh->bts", query_head, self_pair[:, :, 0], preferred_element_type=jnp.float32
            )
            * score_scale
        )
        near_scores = jnp.where(allowed, near_scores, -jnp.inf)
        row_top = jnp.maximum(
            jnp.max(far_scores, axis=1).reshape(blocks, slot_count), jnp.max(near_scores, axis=2)
        )
        far_weight = jnp.exp(far_scores - row_top.reshape(row_count, 1))
        near_weight = jnp.exp(near_scores - row_top[:, :, None])
        weight_total = jnp.sum(far_weight, axis=1).reshape(blocks, slot_count) + jnp.sum(
            near_weight, axis=2
        )
        output = jnp.dot(
            far_weight.astype(jnp.bfloat16), cache_pair[1], preferred_element_type=jnp.float32
        ).reshape(blocks, slot_count, HD)
        output = output + jnp.einsum(
            "bts,bsh->bth",
            near_weight.astype(jnp.bfloat16),
            self_pair[:, :, 1],
            preferred_element_type=jnp.float32,
        )
        output = output / weight_total[:, :, None]
        return jnp.where(valid_rows[:, :, None], output, 0.0).astype(jnp.bfloat16)

    heads_out = lax.map(one_head, jnp.arange(local_heads))
    result = jnp.transpose(heads_out, (1, 2, 0, 3)).reshape(
        sources, item_count, slot_count, head_width
    )
    returned = lax.all_to_all(result, "dp", split_axis=0, concat_axis=0, tiled=True)
    attention_rows = returned.reshape(capacity, slot_count, head_width)[target]
    pooled_local = attention_rows[positions, lengths - 1]
    pooled_all = lax.all_gather(pooled_local, "dp", axis=0, tiled=True)
    partial_mix = jnp.dot(pooled_all, output_weight, preferred_element_type=jnp.float32)
    scaled_head = norm_gain * reward_head
    combined = lax.psum(partial_mix, "mp") + residual.astype(jnp.float32)
    square_sum = jnp.sum(combined * combined, axis=1)
    signal = jnp.sum(combined * scaled_head[None, :], axis=1)
    square_sum, signal = lax.psum((square_sum, signal), "dp")
    inverse = lax.rsqrt(square_sum / D + EPSILON)
    rewards = inverse * signal
    pair_loss, reward_slope = bradley_terry(rewards, pairing)
    direct_term = reward_slope * inverse
    norm_term = reward_slope * inverse * inverse * inverse * signal / D
    upstream = direct_term[:, None] * scaled_head[None, :] - norm_term[:, None] * combined
    head_gradient = jnp.sum(direct_term[:, None] * combined * norm_gain[None, :], axis=0)
    upstream_half = upstream.astype(jnp.bfloat16)
    weight_gradient = lax.dot_general(
        pooled_all, upstream_half, (((0,), (0,)), ((), ())), preferred_element_type=jnp.float32
    )
    pooled_gradient = lax.psum_scatter(
        lax.dot_general(
            upstream_half,
            output_weight,
            (((1,), (1,)), ((), ())),
            preferred_element_type=jnp.float32,
        ),
        "dp",
        scatter_dimension=0,
        tiled=True,
    )
    return (attention_rows, rewards, pair_loss, weight_gradient, head_gradient, pooled_gradient)


def solution(mesh):
    placed = (
        P("dp", None, "mp"),
        P(None, "dp", None, None),
        P(None, "dp", None, None),
        P("dp"),
        P("dp"),
        P(),
        P(None, "dp"),
        P("mp", "dp"),
        P("dp"),
        P("dp"),
    )
    return jax.shard_map(
        shards,
        mesh=mesh,
        in_specs=placed,
        out_specs=(P("dp", None, "mp"), P(), P(), P("mp", "dp"), P("dp"), P("dp", "mp")),
        check_vma=False,
    )
```

profile of v0, /device:TPU:0, one launch (start us, length us, event | category | flops | bytes accessed | tf_op | source)
XLA Modules:
  0.0 529.6 jit_solution(9194661605754231046)
XLA Ops:
  10.4 5.2 all-to-all-start
  18.1 3.6 gather_fusion
  21.8 3.4 select_bitcast_fusion
  26.2 7.2 %scatter_fusion = bf16[48,8,1536]{2,1,0:T(8,128)(2,1)} fusion(bf16[48,8,1536]{2,1,0:T(8,128)(2,1)} %broadcast_in_dim.88, s32[48]{0:T(128)S(1)} %compare_select_fusion.6, bf16[48,8,1536]{2,1,0:T(8,128)(2,1)} %param.12), kind=kCustom, calls=%fused_computation.6 | custom fusion | bytes 3539136 | tf_op jit(solution)/shard_map/scatter | solution.py:68
  33.4 4.2 all-to-all-start.1
  43.2 8.2 %scatter_fusion.1 = bf16[48,8,3072]{2,1,0:T(8,128)(2,1)} fusion(bf16[48,8,3072]{2,1,0:T(8,128)(2,1)} %broadcast_in_dim.89, s32[48]{0:T(128)S(1)} %compare_select_fusion.6, bf16[48,8,3072]{2,1,0:T(8,128)(2,1)} %pad_maximum_fusion), kind=kCustom, calls=%fused_computation.7 | custom fusion | bytes 7078080 | tf_op jit(solution)/shard_map/scatter | solution.py:74
  51.4 3.1 all-to-all-done.1
  54.5 4.4 all-to-all-start.2
  58.9 2.7 dynamic-slice_bitcast_fusion.4
  62.9 25.4 %all-to-all-done.2 = bf16[8,6,8,3072]{3,2,1,0:T(8,128)(2,1)} async-done(((bf16[8,6,8,3072]{3,2,1,0:T(8,128)(2,1)}), bf16[8,6,8,3072]{3,2,1,0:T(8,128)(2,1)}, u32[]{:S(2)}, u32[]{:S(2)}) %all-to-all-start.2) | async-done | bytes 2359328 | tf_op jit(solution)/shard_map/all_to_all | solution.py:82
  88.9 239.0 %while.13 = (s32[]{:T(128)}, bf16[12,48,8,128]{3,2,0,1:T(8,128)(2,1)}, s32[12]{0:T(128)}, bf16[48,8,12,128]{3,1,2,0:T(8,128)(2,1)}, s32[12]{0:T(128)}, /*index=5...) while((s32[]{:T(128)}, ...), condition=%wide.region_9.10_spmd.clone.clone, body=%wide.region_4.9_spmd.clone.clone.sunk | while | flops 205486080 | bytes 6827307 | solution.py:138
  133.8 2.5 fusion.67
  327.9 4.4 all-to-all-start.3
  332.4 16.7 %all-to-all-done.3 = bf16[8,6,8,1536]{3,2,1,0:T(8,128)(2,1)} async-done(((bf16[8,6,8,1536]{3,2,1,0:T(8,128)(2,1)}), bf16[8,6,8,1536]{3,2,1,0:T(8,128)(2,1)}, u32[]{:S(2)}, u32[]{:S(2)}) %all-to-all-start.3) | async-done | bytes 1179680 | tf_op jit(solution)/shard_map/all_to_all | solution.py:142
  349.2 3.0 gather_fusion.1
  352.1 3.2 gather_fusion.2
  355.4 23.5 %all-gather.2.cloned.1.call-done = bf16[384,1536]{1,0:T(8,128)(2,1)} async-done(((bf16[48,1536]{1,0:T(8,128)(2,1)}), bf16[384,1536]{1,0:T(8,128)(2,1)}) %all-gather.2.cloned.1.call-update) | async-done | bytes 1179664 | tf_op jit(solution)/shard_map/all_gather | solution.py:145
  378.9 3.8 fusion.44
  383.9 68.1 %all-reduce.3.cloned.1.call-done = f32[384,1024]{1,0:T(8,128)} async-done(((f32[384,1024]{1,0:T(8,128)}), f32[384,1024]{1,0:T(8,128)}) %all-reduce.3.cloned.1.call-update) | async-done | bytes 1572880 | tf_op jit(solution)/shard_map/psum | solution.py:148
  454.0 12.5 %all-reduce = (f32[384]{0:T(512)S(1)}, f32[384]{0:T(512)S(1)}) all-reduce(f32[384]{0:T(512)S(1)} %get-tuple-element.190, f32[384]{0:T(512)S(1)} %get-tuple-element.189), channel_id=1, replica_groups=mesh['dp'=8,'mp'=4] {'dp'}, use_global_device_ids=true, to_apply=%region_14.15 | all-reduce | flops 768 | bytes 6144 | tf_op jit(solution)/shard_map/psum | solution.py:151
  474.3 2.7 multiply_reduce_fusion
  477.9 2.9 fusion.46
  481.4 6.0 %fusion.45 = f32[1536,1024]{1,0:T(8,128)} fusion(bf16[384,1536]{1,0:T(8,128)(2,1)} %all-gather.2.cloned.1.call-done, bf16[384,1024]{1,0:T(8,128)(2,1)} %copy-done.3), kind=kOutput, calls=%fused_computation.102 | convolution fusion | flops 1207959552 | bytes 8257536 | tf_op jit(solution)/shard_map/dot_general | solution.py:160
  487.5 34.5 %reduce-scatter.2.cloned.1.call-done = f32[48,1536]{1,0:T(8,128)} async-done(((f32[384,1536]{1,0:T(8,128)}), f32[48,1536]{1,0:T(8,128)}) %reduce-scatter.2.cloned.1.call-update) | async-done | bytes 294928 | tf_op jit(solution)/shard_map/reduce_scatter | solution.py:163
  (373 shorter events, 207.2 us)
Async XLA Ops:
  7.2 371.7 %copy-start = (bf16[1536,1024]{1,0:T(8,128)(2,1)S(1)}, bf16[1536,1024]{1,0:T(8,128)(2,1)}, u32[]{:S(2)}) copy-start(bf16[1536,1024]{1,0:T(8,128)(2,1)} %param.19) | copy-start | bytes 9437188
  8.9 34.3 %copy-start.5 = (s32[48]{0:T(128)}, s32[48]{0:T(128)S(1)}, u32[]{:S(2)}) copy-start(s32[48]{0:T(128)S(1)} %compare_select_fusion.6) | copy-start | bytes 580
  10.4 23.0 %all-to-all-start = ((s32[8,1,6]{2,1,0:T(1,128)}), s32[8,1,6]{2,1,0:T(1,128)S(1)}, u32[]{:S(2)}, u32[]{:S(2)}) async-start(s32[8,1,6]{2,1,0:T(1,128)} %bitcast.10), calls=%async_computation | async-start | bytes 8192 | tf_op jit(solution)/shard_map/all_to_all | solution.py:83
  33.4 21.1 %all-to-all-start.1 = ((bf16[8,6,8,1536]{3,2,1,0:T(8,128)(2,1)}), bf16[8,6,8,1536]{3,2,1,0:T(8,128)(2,1)}, u32[]{:S(2)}, u32[]{:S(2)}) async-start(bf16[8,6,8,1536]{3,2,1,0:T(8,128)(2,1)} %bitcast.101), calls=%async_computation.1 | async-start | bytes 2359296 | tf_op jit(solution)/shard_map/all_to_all | solution.py:81
  54.5 33.8 %all-to-all-start.2 = ((bf16[8,6,8,3072]{3,2,1,0:T(8,128)(2,1)}), bf16[8,6,8,3072]{3,2,1,0:T(8,128)(2,1)}, u32[]{:S(2)}, u32[]{:S(2)}) async-start(bf16[8,6,8,3072]{3,2,1,0:T(8,128)(2,1)} %bitcast.100), calls=%async_computation.2 | async-start | bytes 4718592 | tf_op jit(solution)/shard_map/all_to_all | solution.py:82
  102.5 3.2 copy-start.2
  122.4 3.2 copy-start.2
  142.3 3.2 copy-start.2
  162.2 3.2 copy-start.2
  182.2 3.2 copy-start.2
  202.1 3.2 copy-start.2
  222.0 3.2 copy-start.2
  241.9 3.2 copy-start.2
  261.8 3.2 copy-start.2
  281.8 3.2 copy-start.2
  301.7 3.2 copy-start.2
  321.6 3.2 copy-start.2
  327.9 4.4 copy-start.6
  327.9 4.5 copy-start.9
  327.9 21.2 %all-to-all-start.3 = ((bf16[8,6,8,1536]{3,2,1,0:T(8,128)(2,1)}), bf16[8,6,8,1536]{3,2,1,0:T(8,128)(2,1)}, u32[]{:S(2)}, u32[]{:S(2)}) async-start(bf16[8,6,8,1536]{3,2,1,0:T(8,128)(2,1)} %bitcast.12), calls=%async_computation.3 | async-start | bytes 2359296 | tf_op jit(solution)/shard_map/all_to_all | solution.py:142
  332.3 46.6 %all-gather.2.cloned.1.call-start = ((), (), s32[]{:S(2)}) async-start(), calls=%async_computation.5 | async-start | bytes 1327104 | tf_op jit(solution)/shard_map/all_gather | solution.py:145
  355.3 96.7 %all-reduce.3.cloned.1.call-start = ((), (), s32[]{:S(2)}) async-start(), calls=%async_computation.6 | async-start | bytes 3145728 | tf_op jit(solution)/shard_map/psum | solution.py:148
  382.7 139.2 %reduce-scatter.2.cloned.1.call-start = ((), (), s32[]{:S(2)}) async-start(), calls=%async_computation.7 | async-start | bytes 2654208 | tf_op jit(solution)/shard_map/reduce_scatter | solution.py:163
  466.5 7.8 %copy-start.1 = (f32[384]{0:T(512)}, f32[384]{0:T(512)S(1)}, u32[]{:S(2)}) copy-start(f32[384]{0:T(512)S(1)} %fusion.33) | copy-start | bytes 4612
  (4 other events, 3.8 us)
Sparse Core Ops, SparseCore 0:
  355.4 23.4 all-gather.1
  382.9 69.0 all-reduce.2
  480.9 40.9 reduce-scatter.1
where the time goes:
time: 534 us; the launch traced here: 530 us
  waiting for transfers between devices  171 us (32%)
  local copies, waits for them, and re-layouts  116 us (22%)
  matrix products  88.1 us (16%)
  loops' own time  55.3 us (10%)
  other arithmetic  52 us (10%)
  starting transfers between devices  18.3 us (3%)
  between operations  15.7 us (3%)
  blocking collectives  12.5 us (2%)
    psum x1, waiting for transfers between devices, shards(): combined = lax.psum(partial_mix, 'mp') + residual.astype(jnp.float32)  68.1 us
    another operation x1, loops' own time, shards(): heads_out = lax.map(one_head, jnp.arange(local_heads))  55.3 us
    reduce_scatter x1, waiting for transfers between devices, shards(): lax.psum_scatter(lax.dot_general(upstream_half, output_weight, (((1,), (1...  34.5 us
    dot_general x12, matrix products, one_head(): lax.dot_general(flat_query, cache_pair[0], (((1,), (1,)), ((), ())), pref...  30.3 us
    all_to_all x1, waiting for transfers between devices, shards(): lax.all_to_all(key_buffer, 'dp', split_axis=0, concat_axis=0, tiled=True)  25.4 us
    all_gather x1, waiting for transfers between devices, shards(): pooled_all = lax.all_gather(pooled_local, 'dp', axis=0, tiled=True)  23.5 us
    dot_general x12, matrix products, one_head(): jnp.dot(far_weight.astype(jnp.bfloat16), cache_pair[1], preferred_element...  22.2 us
    reduce_sum x12, other arithmetic, one_head(): jnp.sum(far_weight, axis=1).reshape(blocks, slot_count)  21.4 us
  transfers between devices with their start and end apart: 7, of which 6 were waited for; matrix products, arithmetic and copies ran while one was open for 8% of the time, Pallas kernels for 0%

commit v1 on v0

v1 whole, which is shorter than its diff:
```python
import functools
import math

import jax
import jax.numpy as jnp
from jax import lax
from jax.experimental import pallas as pl
from jax.experimental.pallas import tpu as pltpu
from jax.sharding import PartitionSpec as P

D = 8192
HD = 128
Q_HEADS = 48
KV_HEADS = 6


EPSILON = 1e-05


def bradley_terry(rewards, pairing):
    count = rewards.shape[0]
    chosen = pairing[0::2, None] == jnp.arange(count)[None, :]
    rejected = pairing[1::2, None] == jnp.arange(count)[None, :]
    sign = chosen.astype(jnp.float32) - rejected.astype(jnp.float32)
    margin = jnp.sum(sign * rewards[None, :], axis=1)
    loss_value = jnp.mean(jax.nn.softplus(-margin))
    slope = -jax.nn.sigmoid(-margin) / margin.shape[0]
    reward_slope = jnp.sum(sign * slope[:, None], axis=0)
    return (loss_value, reward_slope)


def pack_kernel(window, meta, query, keys, out):
    slots = out.shape[0]
    width = query.shape[2]
    span = window * HD
    first = pl.multiple_of(meta[2 * slots] * HD, HD)

    def body(p, carry):
        r = meta[p]
        out[p, :, pl.ds(0, width)] = query[r]
        out[p, :, pl.ds(width, span)] = keys[0, r, :, pl.ds(first, span)]
        out[p, :, pl.ds(width + span, span)] = keys[1, r, :, pl.ds(first, span)]
        length = meta[slots + p].astype(jnp.float32)
        out[p, :, pl.ds(width + 2 * span, HD)] = jnp.full(
            (out.shape[1], HD), length, jnp.float32
        ).astype(jnp.bfloat16)
        return carry

    lax.fori_loop(0, slots, body, 0)


def attention_kernel(slot_count, meta, query, own_k, own_v, lens, cache, out):
    rows = query.shape[0]
    chunk = 128
    scale = math.log2(math.e) / math.sqrt(HD)
    contract = (((1,), (1,)), ((), ()))
    row = lax.broadcasted_iota(jnp.int32, (chunk, chunk), 0)
    col = lax.broadcasted_iota(jnp.int32, (chunk, chunk), 1)
    t = row % slot_count
    s = col % slot_count
    causal = (row // slot_count == col // slot_count) & (s <= t)
    s_float = s.astype(jnp.float32)
    t_float = t.astype(jnp.float32)
    for start in range(0, rows, chunk):
        here = pl.ds(start, chunk)
        q = query[here, :]
        length = lens[here, :].astype(jnp.float32)
        far = lax.dot_general(q, cache[0, 0], contract, preferred_element_type=jnp.float32)
        near = lax.dot_general(q, own_k[here, :], contract, preferred_element_type=jnp.float32)
        near = jnp.where(causal & (s_float < length), near, -jnp.inf)
        top = jnp.maximum(
            jnp.max(far, axis=1, keepdims=True), jnp.max(near, axis=1, keepdims=True)
        )
        far = jnp.exp2((far - top) * scale)
        near = jnp.exp2((near - top) * scale)
        total = jnp.sum(far, axis=1, keepdims=True) + jnp.sum(near, axis=1, keepdims=True)
        value = jnp.dot(far.astype(jnp.bfloat16), cache[1, 0], preferred_element_type=jnp.float32)
        value += jnp.dot(
            near.astype(jnp.bfloat16), own_v[here, :], preferred_element_type=jnp.float32
        )
        value = jnp.where(t_float < length, value / total, 0.0)
        out[here, :] = value.astype(jnp.bfloat16)


def unpack_kernel(meta, returned, out, pooled, last):
    held, slot_count, width = out.shape
    row = lax.broadcasted_iota(jnp.int32, (slot_count, width), 0)

    def body(r, carry):
        block = returned[meta[r]]
        out[r] = block
        picked = jnp.where(row == meta[held + r] - 1, block.astype(jnp.float32), 0.0)
        last[pl.ds(r, 1), :] = jnp.sum(picked, axis=0, keepdims=True)
        return carry

    lax.fori_loop(0, held, body, 0)
    pooled[...] = last[...].astype(jnp.bfloat16)


def shards(
    response_query,
    response_keys,
    prompt_cache,
    lengths,
    owners,
    pairing,
    residual,
    output_weight,
    norm_gain,
    reward_head,
):
    groups = lax.axis_size("dp")
    planes = lax.axis_size("mp")
    model_rank = lax.axis_index("mp")
    held_count, slot_count, head_width = response_query.shape
    local_heads = head_width // HD
    group_size = Q_HEADS // KV_HEADS
    per_owner = (held_count + groups - 1) // groups
    capacity = groups * per_owner
    window = max(
        (m * local_heads + local_heads - 1) // group_size - m * local_heads // group_size + 1
        for m in range(planes)
    )
    first_head = jnp.minimum(model_rank * local_heads // group_size, KV_HEADS - window)
    head_kv = (model_rank * local_heads + jnp.arange(local_heads)) // group_size
    positions = jnp.arange(held_count)
    earlier = (owners[None, :] == owners[:, None]) & (positions[None, :] < positions[:, None])
    target = (owners * per_owner + jnp.sum(earlier, axis=1)).astype(jnp.int32)
    sent_from = (target[None, :] == jnp.arange(capacity)[:, None]).astype(jnp.int32)
    source = jnp.sum(sent_from * positions[None, :], axis=1)
    slot_length = jnp.sum(sent_from * lengths[None, :], axis=1)
    params = pltpu.CompilerParams(vmem_limit_bytes=40 * 1024 * 1024)
    vmem = pl.BlockSpec(memory_space=pltpu.VMEM)
    smem = pl.BlockSpec(memory_space=pltpu.SMEM)
    packed_width = head_width + (2 * window + 1) * HD
    packed = pl.pallas_call(
        functools.partial(pack_kernel, window),
        out_shape=jax.ShapeDtypeStruct((capacity, slot_count, packed_width), jnp.bfloat16),
        in_specs=[smem, vmem, vmem],
        out_specs=vmem,
        compiler_params=params,
        name="pack",
    )(
        jnp.concatenate([source, slot_length, first_head[None]]).astype(jnp.int32),
        response_query,
        response_keys,
    )
    packed = packed.reshape(groups, per_owner, slot_count, packed_width)
    arrived = lax.all_to_all(packed, "dp", split_axis=0, concat_axis=0, tiled=True)
    rows = capacity * slot_count
    arrived = arrived.reshape(rows, packed_width)
    block = (rows, HD)
    attended = pl.pallas_call(
        functools.partial(attention_kernel, slot_count),
        out_shape=jax.ShapeDtypeStruct((rows, head_width), jnp.bfloat16),
        grid_spec=pltpu.PrefetchScalarGridSpec(
            num_scalar_prefetch=1,
            grid=(local_heads,),
            in_specs=[
                pl.BlockSpec(block, lambda h, meta: (0, h)),
                pl.BlockSpec(block, lambda h, meta: (0, local_heads + meta[local_heads + h])),
                pl.BlockSpec(
                    block, lambda h, meta: (0, local_heads + window + meta[local_heads + h])
                ),
                pl.BlockSpec(block, lambda h, meta: (0, local_heads + 2 * window)),
                pl.BlockSpec(
                    (2, 1, prompt_cache.shape[2], HD), lambda h, meta: (0, 0, 0, meta[h])
                ),
            ],
            out_specs=pl.BlockSpec(block, lambda h, meta: (0, h)),
        ),
        compiler_params=params,
        name="attention",
    )(
        jnp.concatenate([head_kv, head_kv - first_head]).astype(jnp.int32),
        arrived,
        arrived,
        arrived,
        arrived,
        prompt_cache,
    )
    result = attended.reshape(groups, per_owner, slot_count, head_width)
    returned = lax.all_to_all(result, "dp", split_axis=0, concat_axis=0, tiled=True)
    attention_rows, pooled_local = pl.pallas_call(
        unpack_kernel,
        out_shape=(
            jax.ShapeDtypeStruct(response_query.shape, jnp.bfloat16),
            jax.ShapeDtypeStruct((held_count, head_width), jnp.bfloat16),
        ),
        in_specs=[smem, vmem],
        out_specs=(vmem, vmem),
        scratch_shapes=[pltpu.VMEM((held_count, head_width), jnp.float32)],
        compiler_params=params,
        name="unpack",
    )(
        jnp.concatenate([target, lengths]).astype(jnp.int32),
        returned.reshape(capacity, slot_count, head_width),
    )
    pooled_all = lax.all_gather(pooled_local, "dp", axis=0, tiled=True)
    count = pooled_all.shape[0]
    share = count // planes
    partial_mix = jnp.dot(pooled_all, output_weight, preferred_element_type=jnp.float32)
    columns = output_weight.shape[1]
    scaled_head = norm_gain * reward_head
    shares = lax.all_to_all(
        partial_mix.astype(jnp.bfloat16).reshape(planes, share, columns),
        "mp",
        split_axis=0,
        concat_axis=0,
        tiled=True,
    )
    part = jnp.sum(shares.astype(jnp.float32), axis=0) + lax.dynamic_slice_in_dim(
        residual, model_rank * share, share, 0
    ).astype(jnp.float32)
    combined = lax.all_gather(part.astype(jnp.bfloat16), "mp", axis=0, tiled=True).astype(
        jnp.float32
    )
    sums = jnp.stack([jnp.sum(part * part, axis=1), jnp.sum(part * scaled_head[None, :], axis=1)])
    sums = lax.dynamic_update_slice(
        jnp.zeros((2, count), jnp.float32), sums, (jnp.int32(0), model_rank * share)
    )
    square_sum, signal = lax.psum(sums, ("dp", "mp"))
    inverse = lax.rsqrt(square_sum / D + EPSILON)
    rewards = inverse * signal
    pair_loss, reward_slope = bradley_terry(rewards, pairing)
    direct_term = reward_slope * inverse
    norm_term = reward_slope * inverse * inverse * inverse * signal / D
    upstream = direct_term[:, None] * scaled_head[None, :] - norm_term[:, None] * combined
    head_gradient = jnp.sum(direct_term[:, None] * combined * norm_gain[None, :], axis=0)
    upstream_half = upstream.astype(jnp.bfloat16)
    slope_part = lax.dot_general(
        upstream_half,
        output_weight,
        (((1,), (1,)), ((), ())),
        preferred_element_type=jnp.float32,
    ).astype(jnp.bfloat16)
    slope_parts = lax.all_to_all(
        slope_part.reshape(groups, held_count, head_width),
        "dp",
        split_axis=0,
        concat_axis=0,
        tiled=True,
    )
    weight_gradient = lax.dot_general(
        pooled_all, upstream_half, (((0,), (0,)), ((), ())), preferred_element_type=jnp.float32
    )
    pooled_gradient = jnp.sum(slope_parts.astype(jnp.float32), axis=0)
    return (attention_rows, rewards, pair_loss, weight_gradient, head_gradient, pooled_gradient)


def solution(mesh):
    placed = (
        P("dp", None, "mp"),
        P(None, "dp", None, None),
        P(None, "dp", None, None),
        P("dp"),
        P("dp"),
        P(),
        P(None, "dp"),
        P("mp", "dp"),
        P("dp"),
        P("dp"),
    )
    return jax.shard_map(
        shards,
        mesh=mesh,
        in_specs=placed,
        out_specs=(P("dp", None, "mp"), P(), P(), P("mp", "dp"), P("dp"), P("dp", "mp")),
        check_vma=False,
    )
```

time: 534 us -> 237 us (0.44)
  local copies, waits for them, and re-layouts: 116 us -> 7.25 us
  waiting for transfers between devices: 171 us -> 91.2 us
  matrix products: 88.1 us -> 13.4 us
  loops' own time: 55.3 us -> 0 us
  blocking collectives: 12.5 us -> 55.9 us
  other arithmetic: 52 us -> 10.9 us
  Pallas kernels: 0 us -> 23.1 us
    dot_general x48 -> x0, matrix products: 75.5 us -> none  [the longest x12 30.3 us: one_head(): lax.dot_general(flat_query, cache_pair[0], (((1,), (1,)), ((), ())), pref...]
    psum x1 -> x0, waiting for transfers between devices: 68.1 us -> none  [shards(): combined = lax.psum(partial_mix, 'mp') + residual.astype(jnp.float32)]
    another operation x1 -> x0, loops' own time: 55.3 us -> none  [shards(): heads_out = lax.map(one_head, jnp.arange(local_heads))]
    dynamic_slice x37 -> x0, local copies, waits for them, and re-layouts: 47.5 us -> none  [the longest x12 15.1 us: one_head(): head_slot[head_index] * HD]
    reduce_scatter x1 -> x0, waiting for transfers between devices: 34.5 us -> none  [shards(): lax.psum_scatter(lax.dot_general(upstream_half, output_weight, (((1,), (1...]
    psum x1, blocking collectives: 12.5 us -> 37.8 us  [shards(): square_sum, signal = lax.psum(sums, ('dp', 'mp'))]
    pallas_call x0 -> x3, Pallas kernels: none -> 23.1 us  [the longest x1 18.6 us: shards(): pl.pallas_call(functools.partial(attention_kernel, slot_count), out_shape...]
    all_to_all x3, waiting for transfers between devices: 28.6 us -> 50.4 us  [the longest x1 22.1 us: shards(): lax.all_to_all(packed, 'dp', split_axis=0, concat_axis=0, tiled=True)]
  transfers between devices with their start and end apart: 7 -> 5, of which waited for: 6 -> 5; matrix products, arithmetic and copies ran while one was open for 8% -> 4% of each run, Pallas kernels for 0% -> 0%
where the time goes in v1:
time: 237 us; the launch traced here: 236 us
  waiting for transfers between devices  91.2 us (38%)
  blocking collectives  55.9 us (24%)
  Pallas kernels  23.1 us (10%)
  starting transfers between devices  18.8 us (8%)
  between operations  15.9 us (7%)
  matrix products  13.4 us (6%)
  other arithmetic  10.9 us (5%)
  local copies, waits for them, and re-layouts  7.25 us (3%)
    psum x1, blocking collectives, shards(): square_sum, signal = lax.psum(sums, ('dp', 'mp'))  37.8 us
    all_gather x1, waiting for transfers between devices, shards(): pooled_all = lax.all_gather(pooled_local, 'dp', axis=0, tiled=True)  24.1 us
    all_to_all x1, waiting for transfers between devices, shards(): lax.all_to_all(packed, 'dp', split_axis=0, concat_axis=0, tiled=True)  22.1 us
    all_to_all x1, waiting for transfers between devices, shards(): lax.all_to_all(partial_mix.astype(jnp.bfloat16).reshape(planes, share, co...  20.2 us
    pallas_call x1, Pallas kernels, shards(): pl.pallas_call(functools.partial(attention_kernel, slot_count), out_shape...  18.6 us
    all_gather x1, blocking collectives, shards(): lax.all_gather(part.astype(jnp.bfloat16), 'mp', axis=0, tiled=True)  18.1 us
    all_to_all x1, waiting for transfers between devices, shards(): lax.all_to_all(result, 'dp', split_axis=0, concat_axis=0, tiled=True)  16.7 us
    all_to_all x1, waiting for transfers between devices, shards(): lax.all_to_all(slope_part.reshape(groups, held_count, head_width), 'dp',...  8.13 us
  transfers between devices with their start and end apart: 5, of which 5 were waited for; matrix products, arithmetic and copies ran while one was open for 4% of the time, Pallas kernels for 0%

profile of v1, /device:TPU:0, one launch (start us, length us, event | category | flops | bytes accessed | tf_op | source)
XLA Modules:
  0.0 236.4 jit_solution(16269128805024720732)
XLA Ops:
  9.7 1.3 copy-done.4
  11.0 1.3 copy-done.5
  13.2 1.2 copy-done.1
  14.4 5.2 %all-to-all-start = ((bf16[8,6,8,2176]{3,2,1,0:T(8,128)(2,1)}), bf16[8,6,8,2176]{3,2,1,0:T(8,128)(2,1)}, u32[]{:S(2)}, u32[]{:S(2)}) async-start(bf16[8,6,8,2176]{3,2,1,0:T(8,128)(2,1)} %bitcast.13), calls=%async_computation | async-start | bytes 3342336 | tf_op jit(solution)/shard_map/all_to_all | solution.py:149
  19.6 22.1 %all-to-all-done = bf16[8,6,8,2176]{3,2,1,0:T(8,128)(2,1)} async-done(((bf16[8,6,8,2176]{3,2,1,0:T(8,128)(2,1)}), bf16[8,6,8,2176]{3,2,1,0:T(8,128)(2,1)}, u32[]{:S(2)}, u32[]{:S(2)}) %all-to-all-start) | async-done | bytes 1671200 | tf_op jit(solution)/shard_map/all_to_all | solution.py:149
  41.7 1.9 copy-done.3
  43.6 18.6 %attention.1 = bf16[384,1536]{1,0:T(8,128)(2,1)S(1)} custom-call(s32[24]{0:T(128)S(1)} %pad_add_fusion.1.meta, bf16[384,2176]{1,0:T(8,128)(2,1)} %bitcast.2.query.own_k.own_v.lens, bf16[384,2176]{1,0:T(8,128)(2,1)} %bitcast.2.query.own_k.own_v.lens, bf16[384,2176]{1,0:T(8,128)(2,1)} %bitcast.2.query.own_k.own_v.lens, ...), custom_call_target="tpu_custom_call" | custom-call | tf_op jit(solution)/shard_map/attention/pallas_call | solution.py:153
  63.2 4.4 %all-to-all-start.1 = ((bf16[8,6,8,1536]{3,2,1,0:T(8,128)(2,1)}), bf16[8,6,8,1536]{3,2,1,0:T(8,128)(2,1)}, u32[]{:S(2)}, u32[]{:S(2)}) async-start(bf16[8,6,8,1536]{3,2,1,0:T(8,128)(2,1)} %bitcast.14), calls=%async_computation.1 | async-start | bytes 2359296 | tf_op jit(solution)/shard_map/all_to_all | solution.py:183
  67.8 16.7 %all-to-all-done.1 = bf16[8,6,8,1536]{3,2,1,0:T(8,128)(2,1)} async-done(((bf16[8,6,8,1536]{3,2,1,0:T(8,128)(2,1)}), bf16[8,6,8,1536]{3,2,1,0:T(8,128)(2,1)}, u32[]{:S(2)}, u32[]{:S(2)}) %all-to-all-start.1) | async-done | bytes 1179680 | tf_op jit(solution)/shard_map/all_to_all | solution.py:183
  84.4 3.6 %unpack.1 = (bf16[48,8,1536]{2,1,0:T(8,128)(2,1)}, bf16[48,1536]{1,0:T(8,128)(2,1)}) custom-call(s32[96]{0:T(128)S(1)} %pad_add_fusion.meta, bf16[48,8,1536]{2,1,0:T(8,128)(2,1)} %bitcast.4.returned), custom_call_target="tpu_custom_call" | custom-call | tf_op jit(solution)/shard_map/unpack/pallas_call | solution.py:184
  88.0 24.1 %all-gather.2.cloned.1.call-done = bf16[384,1536]{1,0:T(8,128)(2,1)} async-done(((bf16[48,1536]{1,0:T(8,128)(2,1)}), bf16[384,1536]{1,0:T(8,128)(2,1)}) %all-gather.2.cloned.1.call-update) | async-done | bytes 1179664 | tf_op jit(solution)/shard_map/all_gather | solution.py:199
  112.1 3.5 %convolution_convert_fusion.1 = bf16[384,1024]{1,0:T(8,128)(2,1)} fusion(bf16[384,1536]{1,0:T(8,128)(2,1)} %all-gather.2.cloned.1.call-done, bf16[1536,1024]{1,0:T(8,128)(2,1)S(1)} %copy-done), kind=kOutput, calls=%fused_computation.9 | convolution fusion | flops 1208352768 | bytes 5111808 | tf_op jit(solution)/shard_map/dot_general | solution.py:202
  115.7 4.7 %all-to-all-start.2 = ((bf16[4,96,1024]{2,1,0:T(8,128)(2,1)}), bf16[4,96,1024]{2,1,0:T(8,128)(2,1)}, u32[]{:S(2)}, u32[]{:S(2)}) async-start(bf16[4,96,1024]{2,1,0:T(8,128)(2,1)} %bitcast.16), calls=%async_computation.2 | async-start | bytes 1572864 | tf_op jit(solution)/shard_map/all_to_all | solution.py:205
  120.9 20.2 %all-to-all-done.2 = bf16[4,96,1024]{2,1,0:T(8,128)(2,1)} async-done(((bf16[4,96,1024]{2,1,0:T(8,128)(2,1)}), bf16[4,96,1024]{2,1,0:T(8,128)(2,1)}, u32[]{:S(2)}, u32[]{:S(2)}) %all-to-all-start.2) | async-done | bytes 786464 | tf_op jit(solution)/shard_map/all_to_all | solution.py:205
  141.1 1.3 convert_reduce_fusion.1
  142.4 1.1 multiply_reduce_fusion.1
  143.5 18.1 %all_gather.7 = bf16[384,1024]{1,0:T(8,128)(2,1)} all-gather(bf16[96,1024]{1,0:T(8,128)(2,1)S(1)} %get-tuple-element.19), channel_id=1, replica_groups=mesh['dp'=8,'mp'=4] {'mp'}, dimensions={0}, use_global_device_ids=true | all-gather | bytes 983040 | tf_op jit(solution)/shard_map/all_gather | solution.py:215
  161.7 37.8 %psum.7 = f32[2,384]{1,0:T(2,128)S(1)} all-reduce(f32[2,384]{1,0:T(2,128)S(1)} %dynamic_update_slice.3), channel_id=1, replica_groups=mesh['dp'=8,'mp'=4] {'dp','mp'}, use_global_device_ids=true, to_apply=%region_6.7 | all-reduce | flops 768 | bytes 6144 | tf_op jit(solution)/shard_map/psum | solution.py:222
  201.2 3.7 %convolution_convert_fusion = bf16[384,1536]{1,0:T(8,128)(2,1)} fusion(bf16[1536,1024]{1,0:T(8,128)(2,1)S(1)} %copy-done, bf16[384,1024]{1,0:T(8,128)(2,1)} %all_gather.7, f32[384]{0:T(512)S(1)} %get-tuple-element.17, f32[1024]{0:T(1024)S(1)} %mul.141, f32[384]{0:T(512)S(1)} %get-tuple-element.18), kind=kOutput, calls=%fused_computation | convolution fusion | flops 1210515456 | bytes 5118976 | tf_op jit(solution)/shard_map/dot_general | solution.py:231
  204.9 4.5 %all-to-all-start.3 = ((bf16[8,48,1536]{2,1,0:T(8,128)(2,1)}), bf16[8,48,1536]{2,1,0:T(8,128)(2,1)}, u32[]{:S(2)}, u32[]{:S(2)}) async-start(bf16[8,48,1536]{2,1,0:T(8,128)(2,1)} %bitcast.15), calls=%async_computation.3 | async-start | bytes 2359296 | tf_op jit(solution)/shard_map/all_to_all | solution.py:237
  210.0 2.0 fusion.3
  212.0 6.1 %fusion.13 = f32[1536,1024]{1,0:T(8,128)} fusion(bf16[384,1536]{1,0:T(8,128)(2,1)} %all-gather.2.cloned.1.call-done, bf16[384,1024]{1,0:T(8,128)(2,1)} %all_gather.7, f32[384]{0:T(512)S(1)} %get-tuple-element.17, f32[1024]{0:T(1024)S(1)} %mul.141, f32[384]{0:T(512)S(1)} %get-tuple-element.18), kind=kOutput, calls=%fused_computation.47 | convolution fusion | flops 1209925632 | bytes 8264704 | tf_op jit(solution)/shard_map/dot_general | solution.py:244
  218.2 8.1 %all-to-all-done.3 = bf16[8,48,1536]{2,1,0:T(8,128)(2,1)} async-done(((bf16[8,48,1536]{2,1,0:T(8,128)(2,1)}), bf16[8,48,1536]{2,1,0:T(8,128)(2,1)}, u32[]{:S(2)}, u32[]{:S(2)}) %all-to-all-start.3) | async-done | bytes 1179680 | tf_op jit(solution)/shard_map/all_to_all | solution.py:237
  226.3 2.2 convert_reduce_fusion
  (37 shorter events, 6.9 us)
Async XLA Ops:
  7.2 105.0 %copy-start = (bf16[1536,1024]{1,0:T(8,128)(2,1)S(1)}, bf16[1536,1024]{1,0:T(8,128)(2,1)}, u32[]{:S(2)}) copy-start(bf16[1536,1024]{1,0:T(8,128)(2,1)} %param.17) | copy-start | bytes 9437188
  9.7 1.3 copy-start.4
  11.0 1.3 copy-start.5
  13.2 1.2 copy-start.1
  14.4 27.4 %all-to-all-start = ((bf16[8,6,8,2176]{3,2,1,0:T(8,128)(2,1)}), bf16[8,6,8,2176]{3,2,1,0:T(8,128)(2,1)}, u32[]{:S(2)}, u32[]{:S(2)}) async-start(bf16[8,6,8,2176]{3,2,1,0:T(8,128)(2,1)} %bitcast.13), calls=%async_computation | async-start | bytes 3342336 | tf_op jit(solution)/shard_map/all_to_all | solution.py:149
  41.7 1.9 copy-start.3
  62.2 1.0 copy-start.2
  63.2 4.4 %copy-start.9 = (s32[48]{0:T(128)S(1)}, s32[48]{0:T(128)}, u32[]{:S(2)}) copy-start(s32[48]{0:T(128)} %param.13) | copy-start | bytes 580
  63.2 21.2 %all-to-all-start.1 = ((bf16[8,6,8,1536]{3,2,1,0:T(8,128)(2,1)}), bf16[8,6,8,1536]{3,2,1,0:T(8,128)(2,1)}, u32[]{:S(2)}, u32[]{:S(2)}) async-start(bf16[8,6,8,1536]{3,2,1,0:T(8,128)(2,1)} %bitcast.14), calls=%async_computation.1 | async-start | bytes 2359296 | tf_op jit(solution)/shard_map/all_to_all | solution.py:183
  67.6 44.5 %all-gather.2.cloned.1.call-start = ((), (), s32[]{:S(2)}) async-start(), calls=%async_computation.4 | async-start | bytes 1327104 | tf_op jit(solution)/shard_map/all_gather | solution.py:199
  115.7 4.7 %copy-start.8 = (s32[384]{0:T(512)S(1)}, s32[384]{0:T(512)}, u32[]{:S(2)}) copy-start(s32[384]{0:T(512)} %param.15) | copy-start | bytes 4612
  115.7 5.2 %copy-start.6 = (f32[1024]{0:T(1024)S(1)}, f32[1024]{0:T(1024)}, u32[]{:S(2)}) copy-start(f32[1024]{0:T(1024)} %param.18) | copy-start | bytes 12292
  115.7 5.2 %copy-start.7 = (f32[1024]{0:T(1024)S(1)}, f32[1024]{0:T(1024)}, u32[]{:S(2)}) copy-start(f32[1024]{0:T(1024)} %param.19) | copy-start | bytes 12292
  115.7 25.4 %all-to-all-start.2 = ((bf16[4,96,1024]{2,1,0:T(8,128)(2,1)}), bf16[4,96,1024]{2,1,0:T(8,128)(2,1)}, u32[]{:S(2)}, u32[]{:S(2)}) async-start(bf16[4,96,1024]{2,1,0:T(8,128)(2,1)} %bitcast.16), calls=%async_computation.2 | async-start | bytes 1572864 | tf_op jit(solution)/shard_map/all_to_all | solution.py:205
  204.9 21.4 %all-to-all-start.3 = ((bf16[8,48,1536]{2,1,0:T(8,128)(2,1)}), bf16[8,48,1536]{2,1,0:T(8,128)(2,1)}, u32[]{:S(2)}, u32[]{:S(2)}) async-start(bf16[8,48,1536]{2,1,0:T(8,128)(2,1)} %bitcast.15), calls=%async_computation.3 | async-start | bytes 2359296 | tf_op jit(solution)/shard_map/all_to_all | solution.py:237
Sparse Core Ops, SparseCore 0:
  88.2 23.9 all-gather.1

commit v2 on v1

--- a/solution.py
+++ b/solution.py
@@ -41,17 +41,21 @@
         out[p, :, pl.ds(width, span)] = keys[0, r, :, pl.ds(first, span)]
         out[p, :, pl.ds(width + span, span)] = keys[1, r, :, pl.ds(first, span)]
         length = meta[slots + p].astype(jnp.float32)
-        out[p, :, pl.ds(width + 2 * span, HD)] = jnp.full(
-            (out.shape[1], HD), length, jnp.float32
-        ).astype(jnp.bfloat16)
+        place = r.astype(jnp.float32)
+        lane = lax.broadcasted_iota(jnp.int32, (out.shape[1], HD), 1)
+        out[p, :, pl.ds(width + 2 * span, HD)] = jnp.where(lane < HD // 2, length, place).astype(
+            jnp.bfloat16
+        )
         return carry
 
     lax.fori_loop(0, slots, body, 0)
 
 
-def attention_kernel(slot_count, meta, query, own_k, own_v, lens, cache, out):
+def attention_kernel(slot_count, meta, query, own_k, own_v, lens, cache, out, pooled):
     rows = query.shape[0]
+    head = pl.program_id(0)
     chunk = 128
+    blocks = chunk // slot_count
     scale = math.log2(math.e) / math.sqrt(HD)
     contract = (((1,), (1,)), ((), ()))
     row = lax.broadcasted_iota(jnp.int32, (chunk, chunk), 0)
@@ -64,7 +68,7 @@
     for start in range(0, rows, chunk):
         here = pl.ds(start, chunk)
         q = query[here, :]
-        length = lens[here, :].astype(jnp.float32)
+        length = jnp.broadcast_to(lens[here, :].astype(jnp.float32)[:, 0:1], (chunk, chunk))
         far = lax.dot_general(q, cache[0, 0], contract, preferred_element_type=jnp.float32)
         near = lax.dot_general(q, own_k[here, :], contract, preferred_element_type=jnp.float32)
         near = jnp.where(causal & (s_float < length), near, -jnp.inf)
@@ -80,21 +84,25 @@
         )
         value = jnp.where(t_float < length, value / total, 0.0)
         out[here, :] = value.astype(jnp.bfloat16)
-
-
-def unpack_kernel(meta, returned, out, pooled, last):
-    held, slot_count, width = out.shape
-    row = lax.broadcasted_iota(jnp.int32, (slot_count, width), 0)
-
+        last = jnp.where(t_float == length - 1.0, value, 0.0)
+        last = jnp.sum(last.reshape(blocks, slot_count, HD), axis=1)
+        there = pl.ds(start // slot_count, blocks)
+        pooled[there, pl.ds(pl.multiple_of(head * HD, HD), HD)] = last.astype(jnp.bfloat16)
+
+        @pl.when(head == 0)
+        def _():
+            place = lens[here, :].astype(jnp.float32).reshape(blocks, slot_count, HD)
+            pooled[there, pl.ds(pooled.shape[1] - HD, HD)] = jnp.max(place, axis=1).astype(
+                jnp.bfloat16
+            )
+
+
+def unpack_kernel(meta, returned, out):
     def body(r, carry):
-        block = returned[meta[r]]
-        out[r] = block
-        picked = jnp.where(row == meta[held + r] - 1, block.astype(jnp.float32), 0.0)
-        last[pl.ds(r, 1), :] = jnp.sum(picked, axis=0, keepdims=True)
+        out[r] = returned[meta[r]]
         return carry
 
-    lax.fori_loop(0, held, body, 0)
-    pooled[...] = last[...].astype(jnp.bfloat16)
+    lax.fori_loop(0, out.shape[0], body, 0)
 
 
 def shards(
@@ -150,9 +158,12 @@
     rows = capacity * slot_count
     arrived = arrived.reshape(rows, packed_width)
     block = (rows, HD)
-    attended = pl.pallas_call(
+    attended, pooled_sent = pl.pallas_call(
         functools.partial(attention_kernel, slot_count),
-        out_shape=jax.ShapeDtypeStruct((rows, head_width), jnp.bfloat16),
+        out_shape=(
+            jax.ShapeDtypeStruct((rows, head_width), jnp.bfloat16),
+            jax.ShapeDtypeStruct((capacity, head_width + HD), jnp.bfloat16),
+        ),
         grid_spec=pltpu.PrefetchScalarGridSpec(
             num_scalar_prefetch=1,
             grid=(local_heads,),
@@ -167,7 +178,10 @@
                     (2, 1, prompt_cache.shape[2], HD), lambda h, meta: (0, 0, 0, meta[h])
                 ),
             ],
-            out_specs=pl.BlockSpec(block, lambda h, meta: (0, h)),
+            out_specs=(
+                pl.BlockSpec(block, lambda h, meta: (0, h)),
+                pl.BlockSpec((capacity, head_width + HD), lambda h, meta: (0, 0)),
+            ),
         ),
         compiler_params=params,
         name="attention",
@@ -179,25 +193,26 @@
         arrived,
         prompt_cache,
     )
+    pooled_slots = lax.all_gather(pooled_sent, "dp", axis=0, tiled=True)
     result = attended.reshape(groups, per_owner, slot_count, head_width)
     returned = lax.all_to_all(result, "dp", split_axis=0, concat_axis=0, tiled=True)
-    attention_rows, pooled_local = pl.pallas_call(
+    attention_rows = pl.pallas_call(
         unpack_kernel,
-        out_shape=(
-            jax.ShapeDtypeStruct(response_query.shape, jnp.bfloat16),
-            jax.ShapeDtypeStruct((held_count, head_width), jnp.bfloat16),
-        ),
+        out_shape=jax.ShapeDtypeStruct(response_query.shape, jnp.bfloat16),
         in_specs=[smem, vmem],
-        out_specs=(vmem, vmem),
-        scratch_shapes=[pltpu.VMEM((held_count, head_width), jnp.float32)],
+        out_specs=vmem,
         compiler_params=params,
         name="unpack",
-    )(
-        jnp.concatenate([target, lengths]).astype(jnp.int32),
-        returned.reshape(capacity, slot_count, head_width),
-    )
-    pooled_all = lax.all_gather(pooled_local, "dp", axis=0, tiled=True)
-    count = pooled_all.shape[0]
+    )(target, returned.reshape(capacity, slot_count, head_width))
+    count = held_count * groups
+    sender = jnp.arange(capacity * groups) % capacity // per_owner
+    place = pooled_slots[:, head_width + HD - 1].astype(jnp.int32)
+    live = pooled_slots[:, head_width] > 0
+    response = jnp.where(live, sender * held_count + place, count)
+    order = (jnp.arange(count)[:, None] == response[None, :]).astype(jnp.bfloat16)
+    pooled_all = jnp.dot(
+        order, pooled_slots[:, :head_width], preferred_element_type=jnp.float32
+    ).astype(jnp.bfloat16)
     share = count // planes
     partial_mix = jnp.dot(pooled_all, output_weight, preferred_element_type=jnp.float32)
     columns = output_weight.shape[1]
@@ -215,11 +230,9 @@
     combined = lax.all_gather(part.astype(jnp.bfloat16), "mp", axis=0, tiled=True).astype(
         jnp.float32
     )
-    sums = jnp.stack([jnp.sum(part * part, axis=1), jnp.sum(part * scaled_head[None, :], axis=1)])
-    sums = lax.dynamic_update_slice(
-        jnp.zeros((2, count), jnp.float32), sums, (jnp.int32(0), model_rank * share)
-    )
-    square_sum, signal = lax.psum(sums, ("dp", "mp"))
+    square_sum = jnp.sum(combined * combined, axis=1)
+    signal = jnp.sum(combined * scaled_head[None, :], axis=1)
+    square_sum, signal = lax.psum((square_sum, signal), "dp")
     inverse = lax.rsqrt(square_sum / D + EPSILON)
     rewards = inverse * signal
     pair_loss, reward_slope = bradley_terry(rewards, pairing)

time: 237 us -> 201 us (0.85)
  blocking collectives: 55.9 us -> 30.5 us
  waiting for transfers between devices: 91.2 us -> 72.1 us
  Pallas kernels: 23.1 us -> 28.4 us
    psum x1, blocking collectives: 37.8 us -> 12.5 us  [shards(): square_sum, signal = lax.psum((square_sum, signal), 'dp')]
    all_to_all x1, waiting for transfers between devices: 16.7 us -> 0.01 us  [shards(): lax.all_to_all(result, 'dp', split_axis=0, concat_axis=0, tiled=True)]
    pallas_call x1, Pallas kernels: 18.6 us -> 24.8 us  [shards(): pl.pallas_call(functools.partial(attention_kernel, slot_count), out_shape...]
    all_to_all x1, waiting for transfers between devices: 8.13 us -> 5.38 us  [shards(): lax.all_to_all(slope_part.reshape(groups, held_count, head_width), 'dp',...]
    unnamed x20 -> x24, local copies, waits for them, and re-layouts: 6.64 us -> 7.54 us
  transfers between devices with their start and end apart: 5 -> 5, of which waited for: 5 -> 4; matrix products, arithmetic and copies ran while one was open for 4% -> 8% of each run, Pallas kernels for 0% -> 1%
where the time goes in v2:
time: 201 us; the launch traced here: 200 us
  waiting for transfers between devices  72.1 us (36%)
  blocking collectives  30.5 us (15%)
  Pallas kernels  28.4 us (14%)
  starting transfers between devices  18.5 us (9%)
  between operations  16 us (8%)
  matrix products  14.2 us (7%)
  other arithmetic  12.6 us (6%)
  local copies, waits for them, and re-layouts  7.99 us (4%)
    pallas_call x1, Pallas kernels, shards(): pl.pallas_call(functools.partial(attention_kernel, slot_count), out_shape...  24.8 us
    all_gather x1, waiting for transfers between devices, shards(): pooled_slots = lax.all_gather(pooled_sent, 'dp', axis=0, tiled=True)  24.5 us
    all_to_all x1, waiting for transfers between devices, shards(): lax.all_to_all(packed, 'dp', split_axis=0, concat_axis=0, tiled=True)  22 us
    all_to_all x1, waiting for transfers between devices, shards(): lax.all_to_all(partial_mix.astype(jnp.bfloat16).reshape(planes, share, co...  20.2 us
    all_gather x1, blocking collectives, shards(): lax.all_gather(part.astype(jnp.bfloat16), 'mp', axis=0, tiled=True)  18 us
    psum x1, blocking collectives, shards(): square_sum, signal = lax.psum((square_sum, signal), 'dp')  12.5 us
    unnamed x24, local copies, waits for them, and re-layouts  7.54 us
    dot_general x1, matrix products, shards(): lax.dot_general(pooled_all, upstream_half, (((0,), (0,)), ((), ())), pref...  6.14 us
  transfers between devices with their start and end apart: 5, of which 4 were waited for; matrix products, arithmetic and copies ran while one was open for 8% of the time, Pallas kernels for 1%

profile of v2, /device:TPU:0, one launch (start us, length us, event | category | flops | bytes accessed | tf_op | source)
XLA Modules:
  0.0 200.2 jit_solution(14153715350597600624)
XLA Ops:
  9.7 1.3 copy-done.4
  11.0 1.3 copy-done.5
  13.2 1.2 copy-done.1
  14.4 5.2 %all-to-all-start = ((bf16[8,6,8,2176]{3,2,1,0:T(8,128)(2,1)}), bf16[8,6,8,2176]{3,2,1,0:T(8,128)(2,1)}, u32[]{:S(2)}, u32[]{:S(2)}) async-start(bf16[8,6,8,2176]{3,2,1,0:T(8,128)(2,1)} %bitcast.11), calls=%async_computation | async-start | bytes 3342336 | tf_op jit(solution)/shard_map/all_to_all | solution.py:157
  19.7 22.0 %all-to-all-done = bf16[8,6,8,2176]{3,2,1,0:T(8,128)(2,1)} async-done(((bf16[8,6,8,2176]{3,2,1,0:T(8,128)(2,1)}), bf16[8,6,8,2176]{3,2,1,0:T(8,128)(2,1)}, u32[]{:S(2)}, u32[]{:S(2)}) %all-to-all-start) | async-done | bytes 1671200 | tf_op jit(solution)/shard_map/all_to_all | solution.py:157
  41.7 1.9 copy-done.2
  43.6 24.8 %attention.1 = (bf16[384,1536]{1,0:T(8,128)(2,1)S(1)}, bf16[48,1664]{1,0:T(8,128)(2,1)}) custom-call(s32[24]{0:T(128)S(1)} %pad_add_fusion.meta, bf16[384,2176]{1,0:T(8,128)(2,1)} %bitcast.2.query.own_k.own_v.lens, bf16[384,2176]{1,0:T(8,128)(2,1)} %bitcast.2.query.own_k.own_v.lens, bf16[384,2176]{1,0:T(8,128)(2,1)} %bitcast.2.query.own_k.own_v.lens, ...), custom_call_target="tpu_custom_call" | custom-call | tf_op jit(solution)/shard_map/attention/pallas_call | solution.py:161
  69.5 24.5 %all-gather.2.cloned.1.call-done = bf16[384,1664]{1,0:T(8,128)(2,1)} async-done(((bf16[48,1664]{1,0:T(8,128)(2,1)}), bf16[384,1664]{1,0:T(8,128)(2,1)}) %all-gather.2.cloned.1.call-update) | async-done | bytes 1277968 | tf_op jit(solution)/shard_map/all_gather | solution.py:196
  95.0 1.1 convert_reduce_fusion.2
  96.1 2.0 %convolution_convert_fusion.1 = bf16[384,1536]{1,0:T(8,128)(2,1)S(1)} fusion(bf16[384,1664]{1,0:T(8,128)(2,1)} %all-gather.2.cloned.1.call-done, s32[384]{0:T(512)S(1)} %add_select_fusion.2), kind=kOutput, calls=%fused_computation.1 | convolution fusion | flops 453722112 | bytes 2360832 | tf_op jit(solution)/shard_map/dot_general | solution.py:213
  98.2 2.3 %convolution_convert_fusion.2 = bf16[384,1024]{1,0:T(8,128)(2,1)} fusion(bf16[384,1536]{1,0:T(8,128)(2,1)S(1)} %convolution_convert_fusion.1, bf16[1536,1024]{1,0:T(8,128)(2,1)S(1)} %copy-done), kind=kOutput, calls=%fused_computation.14 | convolution fusion | flops 1208352768 | bytes 5111808 | tf_op jit(solution)/shard_map/dot_general | solution.py:217
  100.5 4.7 %all-to-all-start.2 = ((bf16[4,96,1024]{2,1,0:T(8,128)(2,1)}), bf16[4,96,1024]{2,1,0:T(8,128)(2,1)}, u32[]{:S(2)}, u32[]{:S(2)}) async-start(bf16[4,96,1024]{2,1,0:T(8,128)(2,1)} %bitcast.14), calls=%async_computation.2 | async-start | bytes 1572864 | tf_op jit(solution)/shard_map/all_to_all | solution.py:220
  105.7 20.2 %all-to-all-done.2 = bf16[4,96,1024]{2,1,0:T(8,128)(2,1)} async-done(((bf16[4,96,1024]{2,1,0:T(8,128)(2,1)}), bf16[4,96,1024]{2,1,0:T(8,128)(2,1)}, u32[]{:S(2)}, u32[]{:S(2)}) %all-to-all-start.2) | async-done | bytes 786464 | tf_op jit(solution)/shard_map/all_to_all | solution.py:220
  125.9 4.3 %all-to-all-start.1 = ((bf16[8,6,8,1536]{3,2,1,0:T(8,128)(2,1)}), bf16[8,6,8,1536]{3,2,1,0:T(8,128)(2,1)}, u32[]{:S(2)}, u32[]{:S(2)}) async-start(bf16[8,6,8,1536]{3,2,1,0:T(8,128)(2,1)} %bitcast.12), calls=%async_computation.1 | async-start | bytes 2359296 | tf_op jit(solution)/shard_map/all_to_all | solution.py:198
  130.2 1.3 convert_reduce_fusion.1
  132.5 18.0 %all_gather.7 = bf16[384,1024]{1,0:T(8,128)(2,1)S(1)} all-gather(bf16[96,1024]{1,0:T(8,128)(2,1)S(1)} %add_convert_fusion), channel_id=1, replica_groups=mesh['dp'=8,'mp'=4] {'mp'}, dimensions={0}, use_global_device_ids=true | all-gather | bytes 983040 | tf_op jit(solution)/shard_map/all_gather | solution.py:230
  151.7 12.5 %all-reduce = (f32[384]{0:T(512)S(1)}, f32[384]{0:T(512)S(1)}) all-reduce(f32[384]{0:T(512)S(1)} %get-tuple-element.11, f32[384]{0:T(512)S(1)} %get-tuple-element.10), channel_id=1, replica_groups=mesh['dp'=8,'mp'=4] {'dp'}, use_global_device_ids=true, to_apply=%region_7.8 | all-reduce | flops 768 | bytes 6144 | tf_op jit(solution)/shard_map/psum | solution.py:235
  165.3 3.7 %convolution_convert_fusion = bf16[384,1536]{1,0:T(8,128)(2,1)} fusion(bf16[1536,1024]{1,0:T(8,128)(2,1)S(1)} %copy-done, bf16[384,1024]{1,0:T(8,128)(2,1)} %copy-done.6, f32[384]{0:T(512)S(1)} %get-tuple-element.17, f32[384]{0:T(512)S(1)} %get-tuple-element.16, f32[1024]{0:T(1024)S(1)} %mul.123), kind=kOutput, calls=%fused_computation | convolution fusion | flops 1210515456 | bytes 5118976 | tf_op jit(solution)/shard_map/dot_general | solution.py:244
  169.0 4.3 %all-to-all-start.3 = ((bf16[8,48,1536]{2,1,0:T(8,128)(2,1)}), bf16[8,48,1536]{2,1,0:T(8,128)(2,1)}, u32[]{:S(2)}, u32[]{:S(2)}) async-start(bf16[8,48,1536]{2,1,0:T(8,128)(2,1)} %bitcast.13), calls=%async_computation.3 | async-start | bytes 2359296 | tf_op jit(solution)/shard_map/all_to_all | solution.py:250
  173.3 2.6 %unpack.1 = bf16[48,8,1536]{2,1,0:T(8,128)(2,1)} custom-call(s32[48]{0:T(128)S(1)} %multiply_add_fusion.meta, bf16[48,8,1536]{2,1,0:T(8,128)(2,1)} %bitcast.4.returned), custom_call_target="tpu_custom_call" | custom-call | tf_op jit(solution)/shard_map/unpack/pallas_call | solution.py:199
  176.6 2.0 %fusion.5 = f32[1024]{0:T(1024)} fusion(bf16[384,1024]{1,0:T(8,128)(2,1)} %copy-done.6, f32[1024]{0:T(1024)S(1)} %copy-done.8, f32[384]{0:T(512)S(1)} %get-tuple-element.16), kind=kLoop, calls=%fused_computation.12 | loop fusion | flops 1571840 | bytes 796160 | tf_op jit(solution)/shard_map/reduce_sum | solution.py:242
  178.6 6.1 %fusion.19 = f32[1536,1024]{1,0:T(8,128)} fusion(bf16[384,1536]{1,0:T(8,128)(2,1)} %copy-done.7, bf16[384,1024]{1,0:T(8,128)(2,1)} %copy-done.6, f32[384]{0:T(512)S(1)} %get-tuple-element.17, f32[384]{0:T(512)S(1)} %get-tuple-element.16, f32[1024]{0:T(1024)S(1)} %mul.123), kind=kOutput, calls=%fused_computation.59 | convolution fusion | flops 1209925632 | bytes 8264704 | tf_op jit(solution)/shard_map/dot_general | solution.py:257
  184.7 5.4 %all-to-all-done.3 = bf16[8,48,1536]{2,1,0:T(8,128)(2,1)} async-done(((bf16[8,48,1536]{2,1,0:T(8,128)(2,1)}), bf16[8,48,1536]{2,1,0:T(8,128)(2,1)}, u32[]{:S(2)}, u32[]{:S(2)}) %all-to-all-start.3) | async-done | bytes 1179680 | tf_op jit(solution)/shard_map/all_to_all | solution.py:250
  190.1 2.2 %convert_reduce_fusion = f32[48,1536]{1,0:T(8,128)} fusion(bf16[8,48,1536]{2,1,0:T(8,128)(2,1)} %all-to-all-done.3), kind=kLoop, calls=%fused_computation.6 | loop fusion | flops 1105920 | bytes 1474560 | tf_op jit(solution)/shard_map/reduce_sum | solution.py:260
  (42 shorter events, 9.4 us)
Async XLA Ops:
  7.2 91.0 %copy-start = (bf16[1536,1024]{1,0:T(8,128)(2,1)S(1)}, bf16[1536,1024]{1,0:T(8,128)(2,1)}, u32[]{:S(2)}) copy-start(bf16[1536,1024]{1,0:T(8,128)(2,1)} %param.17) | copy-start | bytes 9437188
  9.7 1.3 copy-start.4
  11.0 1.3 copy-start.5
  13.2 1.2 copy-start.1
  14.4 27.4 %all-to-all-start = ((bf16[8,6,8,2176]{3,2,1,0:T(8,128)(2,1)}), bf16[8,6,8,2176]{3,2,1,0:T(8,128)(2,1)}, u32[]{:S(2)}, u32[]{:S(2)}) async-start(bf16[8,6,8,2176]{3,2,1,0:T(8,128)(2,1)} %bitcast.11), calls=%async_computation | async-start | bytes 3342336 | tf_op jit(solution)/shard_map/all_to_all | solution.py:157
  19.5 74.4 %all-gather.2.cloned.1.call-start = ((), (), s32[]{:S(2)}) async-start(), calls=%async_computation.4 | async-start | bytes 1437696 | tf_op jit(solution)/shard_map/all_gather | solution.py:196
  41.7 1.9 copy-start.2
  68.4 1.0 copy-start.3
  98.2 2.3 %copy-start.7 = (bf16[384,1536]{1,0:T(8,128)(2,1)}, bf16[384,1536]{1,0:T(8,128)(2,1)S(1)}, u32[]{:S(2)}) copy-start(bf16[384,1536]{1,0:T(8,128)(2,1)S(1)} %convolution_convert_fusion.1) | copy-start | bytes 3538948
  100.5 4.8 %copy-start.11 = (s32[384]{0:T(512)S(1)}, s32[384]{0:T(512)}, u32[]{:S(2)}) copy-start(s32[384]{0:T(512)} %param.15) | copy-start | bytes 4612
  100.5 5.2 %copy-start.8 = (f32[1024]{0:T(1024)S(1)}, f32[1024]{0:T(1024)}, u32[]{:S(2)}) copy-start(f32[1024]{0:T(1024)} %param.18) | copy-start | bytes 12292
  100.5 5.2 %copy-start.10 = (f32[1024]{0:T(1024)S(1)}, f32[1024]{0:T(1024)}, u32[]{:S(2)}) copy-start(f32[1024]{0:T(1024)} %param.19) | copy-start | bytes 12292
  100.5 25.4 %all-to-all-start.2 = ((bf16[4,96,1024]{2,1,0:T(8,128)(2,1)}), bf16[4,96,1024]{2,1,0:T(8,128)(2,1)}, u32[]{:S(2)}, u32[]{:S(2)}) async-start(bf16[4,96,1024]{2,1,0:T(8,128)(2,1)} %bitcast.14), calls=%async_computation.2 | async-start | bytes 1572864 | tf_op jit(solution)/shard_map/all_to_all | solution.py:220
  125.9 43.1 %all-to-all-start.1 = ((bf16[8,6,8,1536]{3,2,1,0:T(8,128)(2,1)}), bf16[8,6,8,1536]{3,2,1,0:T(8,128)(2,1)}, u32[]{:S(2)}, u32[]{:S(2)}) async-start(bf16[8,6,8,1536]{3,2,1,0:T(8,128)(2,1)} %bitcast.12), calls=%async_computation.1 | async-start | bytes 2359296 | tf_op jit(solution)/shard_map/all_to_all | solution.py:198
  150.5 0.9 copy-start.6
  164.2 4.8 %copy-start.9 = (f32[384]{0:T(512)}, f32[384]{0:T(512)S(1)}, u32[]{:S(2)}) copy-start(f32[384]{0:T(512)S(1)} %fusion.17) | copy-start | bytes 4612
  169.0 21.1 %all-to-all-start.3 = ((bf16[8,48,1536]{2,1,0:T(8,128)(2,1)}), bf16[8,48,1536]{2,1,0:T(8,128)(2,1)}, u32[]{:S(2)}, u32[]{:S(2)}) async-start(bf16[8,48,1536]{2,1,0:T(8,128)(2,1)} %bitcast.13), calls=%async_computation.3 | async-start | bytes 2359296 | tf_op jit(solution)/shard_map/all_to_all | solution.py:250
Sparse Core Ops, SparseCore 0:
  69.6 24.3 all-gather.1

commit v3 on v2

--- a/solution.py
+++ b/solution.py
@@ -29,15 +29,17 @@
     return (loss_value, reward_slope)
 
 
-def pack_kernel(window, meta, query, keys, out):
+def pack_kernel(window, meta, query, keys, out, late):
     slots = out.shape[0]
-    width = query.shape[2]
+    rest = late.shape[2]
+    width = query.shape[2] - rest
     span = window * HD
     first = pl.multiple_of(meta[2 * slots] * HD, HD)
 
     def body(p, carry):
         r = meta[p]
-        out[p, :, pl.ds(0, width)] = query[r]
+        out[p, :, pl.ds(0, width)] = query[r, :, pl.ds(0, width)]
+        late[p] = query[r, :, pl.ds(width, rest)]
         out[p, :, pl.ds(width, span)] = keys[0, r, :, pl.ds(first, span)]
         out[p, :, pl.ds(width + span, span)] = keys[1, r, :, pl.ds(first, span)]
         length = meta[slots + p].astype(jnp.float32)
@@ -51,7 +53,7 @@
     lax.fori_loop(0, slots, body, 0)
 
 
-def attention_kernel(slot_count, meta, query, own_k, own_v, lens, cache, out, pooled):
+def attention_kernel(slot_count, placed, meta, query, own_k, own_v, lens, cache, out, pooled):
     rows = query.shape[0]
     head = pl.program_id(0)
     chunk = 128
@@ -65,6 +67,9 @@
     causal = (row // slot_count == col // slot_count) & (s <= t)
     s_float = s.astype(jnp.float32)
     t_float = t.astype(jnp.float32)
+    gather = lax.broadcasted_iota(jnp.int32, (blocks, chunk), 0)
+    member = lax.broadcasted_iota(jnp.int32, (blocks, chunk), 1)
+    gather = jnp.where(gather == member // slot_count, 1.0, 0.0).astype(jnp.bfloat16)
     for start in range(0, rows, chunk):
         here = pl.ds(start, chunk)
         q = query[here, :]
@@ -85,16 +90,18 @@
         value = jnp.where(t_float < length, value / total, 0.0)
         out[here, :] = value.astype(jnp.bfloat16)
         last = jnp.where(t_float == length - 1.0, value, 0.0)
-        last = jnp.sum(last.reshape(blocks, slot_count, HD), axis=1)
+        last = jnp.dot(gather, last.astype(jnp.bfloat16), preferred_element_type=jnp.float32)
         there = pl.ds(start // slot_count, blocks)
         pooled[there, pl.ds(pl.multiple_of(head * HD, HD), HD)] = last.astype(jnp.bfloat16)
 
-        @pl.when(head == 0)
-        def _():
-            place = lens[here, :].astype(jnp.float32).reshape(blocks, slot_count, HD)
-            pooled[there, pl.ds(pooled.shape[1] - HD, HD)] = jnp.max(place, axis=1).astype(
-                jnp.bfloat16
-            )
+        if placed:
+
+            @pl.when(head == 0)
+            def _():
+                place = lens[here, :].astype(jnp.float32).reshape(blocks, slot_count, HD)
+                pooled[there, pl.ds(pooled.shape[1] - HD, HD)] = jnp.max(place, axis=1).astype(
+                    jnp.bfloat16
+                )
 
 
 def unpack_kernel(meta, returned, out):
@@ -140,12 +147,17 @@
     params = pltpu.CompilerParams(vmem_limit_bytes=40 * 1024 * 1024)
     vmem = pl.BlockSpec(memory_space=pltpu.VMEM)
     smem = pl.BlockSpec(memory_space=pltpu.SMEM)
-    packed_width = head_width + (2 * window + 1) * HD
-    packed = pl.pallas_call(
+    early = local_heads - local_heads // 2
+    late_width = local_heads // 2 * HD
+    packed_width = early * HD + (2 * window + 1) * HD
+    packed, late = pl.pallas_call(
         functools.partial(pack_kernel, window),
-        out_shape=jax.ShapeDtypeStruct((capacity, slot_count, packed_width), jnp.bfloat16),
+        out_shape=(
+            jax.ShapeDtypeStruct((capacity, slot_count, packed_width), jnp.bfloat16),
+            jax.ShapeDtypeStruct((capacity, slot_count, late_width), jnp.bfloat16),
+        ),
         in_specs=[smem, vmem, vmem],
-        out_specs=vmem,
+        out_specs=(vmem, vmem),
         compiler_params=params,
         name="pack",
     )(
@@ -155,45 +167,66 @@
     )
     packed = packed.reshape(groups, per_owner, slot_count, packed_width)
     arrived = lax.all_to_all(packed, "dp", split_axis=0, concat_axis=0, tiled=True)
+    late = late.reshape(groups, per_owner, slot_count, late_width)
+    late = lax.all_to_all(late, "dp", split_axis=0, concat_axis=0, tiled=True)
     rows = capacity * slot_count
+    late = late.reshape(rows, late_width)
     arrived = arrived.reshape(rows, packed_width)
     block = (rows, HD)
-    attended, pooled_sent = pl.pallas_call(
-        functools.partial(attention_kernel, slot_count),
-        out_shape=(
-            jax.ShapeDtypeStruct((rows, head_width), jnp.bfloat16),
-            jax.ShapeDtypeStruct((capacity, head_width + HD), jnp.bfloat16),
-        ),
-        grid_spec=pltpu.PrefetchScalarGridSpec(
-            num_scalar_prefetch=1,
-            grid=(local_heads,),
-            in_specs=[
-                pl.BlockSpec(block, lambda h, meta: (0, h)),
-                pl.BlockSpec(block, lambda h, meta: (0, local_heads + meta[local_heads + h])),
-                pl.BlockSpec(
-                    block, lambda h, meta: (0, local_heads + window + meta[local_heads + h])
+
+    def attend(query, head_base, heads, placed):
+        pooled_width = (heads + placed) * HD
+        at = lambda meta, h: meta[local_heads + head_base + h]
+        return pl.pallas_call(
+            functools.partial(attention_kernel, slot_count, placed),
+            out_shape=(
+                jax.ShapeDtypeStruct((rows, heads * HD), jnp.bfloat16),
+                jax.ShapeDtypeStruct((capacity, pooled_width), jnp.bfloat16),
+            ),
+            grid_spec=pltpu.PrefetchScalarGridSpec(
+                num_scalar_prefetch=1,
+                grid=(heads,),
+                in_specs=[
+                    pl.BlockSpec(block, lambda h, meta: (0, h)),
+                    pl.BlockSpec(block, lambda h, meta: (0, early + at(meta, h))),
+                    pl.BlockSpec(block, lambda h, meta: (0, early + window + at(meta, h))),
+                    pl.BlockSpec(block, lambda h, meta: (0, early + 2 * window)),
+                    pl.BlockSpec(
+                        (2, 1, prompt_cache.shape[2], HD),
+                        lambda h, meta: (0, 0, 0, meta[head_base + h]),
+                    ),
+                ],
+                out_specs=(
+                    pl.BlockSpec(block, lambda h, meta: (0, h)),
+                    pl.BlockSpec((capacity, pooled_width), lambda h, meta: (0, 0)),
                 ),
-                pl.BlockSpec(block, lambda h, meta: (0, local_heads + 2 * window)),
-                pl.BlockSpec(
-                    (2, 1, prompt_cache.shape[2], HD), lambda h, meta: (0, 0, 0, meta[h])
-                ),
-            ],
-            out_specs=(
-                pl.BlockSpec(block, lambda h, meta: (0, h)),
-                pl.BlockSpec((capacity, head_width + HD), lambda h, meta: (0, 0)),
             ),
-        ),
-        compiler_params=params,
-        name="attention",
-    )(
-        jnp.concatenate([head_kv, head_kv - first_head]).astype(jnp.int32),
-        arrived,
-        arrived,
-        arrived,
-        arrived,
-        prompt_cache,
-    )
-    pooled_slots = lax.all_gather(pooled_sent, "dp", axis=0, tiled=True)
+            compiler_params=params,
+            cost_estimate=pl.CostEstimate(
+                flops=4 * rows * heads * HD * prompt_cache.shape[2],
+                bytes_accessed=8 * rows * heads * HD,
+                transcendentals=rows * heads * prompt_cache.shape[2],
+            ),
+            name="attention_early" if placed else "attention_late",
+        )(
+            jnp.concatenate([head_kv, head_kv - first_head]).astype(jnp.int32),
+            query,
+            arrived,
+            arrived,
+            arrived,
+            prompt_cache,
+        )
+
+    def share_rows(own):
+        copies = jnp.broadcast_to(own[None], (groups,) + own.shape)
+        copies = lax.all_to_all(copies, "dp", split_axis=0, concat_axis=0, tiled=True)
+        return copies.reshape(groups * own.shape[0], own.shape[1])
+
+    attended_early, pooled_early = attend(arrived, 0, early, True)
+    pooled_slots = share_rows(pooled_early)
+    attended_late, pooled_late = attend(late, early, local_heads - early, False)
+    pooled_late = share_rows(pooled_late)
+    attended = jnp.concatenate([attended_early, attended_late], axis=1)
     result = attended.reshape(groups, per_owner, slot_count, head_width)
     returned = lax.all_to_all(result, "dp", split_axis=0, concat_axis=0, tiled=True)
     attention_rows = pl.pallas_call(
@@ -206,13 +239,17 @@
     )(target, returned.reshape(capacity, slot_count, head_width))
     count = held_count * groups
     sender = jnp.arange(capacity * groups) % capacity // per_owner
-    place = pooled_slots[:, head_width + HD - 1].astype(jnp.int32)
-    live = pooled_slots[:, head_width] > 0
+    place = pooled_slots[:, early * HD + HD - 1].astype(jnp.int32)
+    live = pooled_slots[:, early * HD] > 0
     response = jnp.where(live, sender * held_count + place, count)
     order = (jnp.arange(count)[:, None] == response[None, :]).astype(jnp.bfloat16)
-    pooled_all = jnp.dot(
-        order, pooled_slots[:, :head_width], preferred_element_type=jnp.float32
-    ).astype(jnp.bfloat16)
+    pooled_all = jnp.concatenate(
+        [
+            jnp.dot(order, slots, preferred_element_type=jnp.float32).astype(jnp.bfloat16)
+            for slots in (pooled_slots[:, : early * HD], pooled_late)
+        ],
+        axis=1,
+    )
     share = count // planes
     partial_mix = jnp.dot(pooled_all, output_weight, preferred_element_type=jnp.float32)
     columns = output_weight.shape[1]

time: 201 us -> 184 us (0.915)
  waiting for transfers between devices: 72.1 us -> 26 us
  blocking collectives: 30.5 us -> 51.4 us
  between operations: 16 us -> 2.61 us
  starting transfers between devices: 18.5 us -> 26.6 us
  local copies, waits for them, and re-layouts: 7.99 us -> 13.6 us
  matrix products: 14.2 us -> 17.3 us
  other arithmetic: 12.6 us -> 15 us
    all_gather x1 -> x0, waiting for transfers between devices: 24.5 us -> none  [shards(): pooled_slots = lax.all_gather(pooled_sent, 'dp', axis=0, tiled=True)]
    all_to_all x0 -> x1, blocking collectives: none -> 20.8 us  [shards(): lax.all_to_all(packed, 'dp', split_axis=0, concat_axis=0, tiled=True)]
    all_to_all x1 -> x3, waiting for transfers between devices: 22 us -> 5.94 us  [the longest x2 5.93 us: share_rows(): lax.all_to_all(copies, 'dp', split_axis=0, concat_axis=0, tiled=True)]
    all_to_all x1 -> x3, starting transfers between devices: 5.17 us -> 12.6 us  [the longest x2 8.39 us: share_rows(): lax.all_to_all(copies, 'dp', split_axis=0, concat_axis=0, tiled=True)]
    all_to_all x1, waiting for transfers between devices: 20.2 us -> 14.7 us  [shards(): lax.all_to_all(partial_mix.astype(jnp.bfloat16).reshape(planes, share, co...]
    unnamed x24 -> x32, local copies, waits for them, and re-layouts: 7.54 us -> 11.4 us
    concatenate x1 -> x2, other arithmetic: 0.08 us -> 2.41 us  [the longest x1 2.34 us: shards(): attended = jnp.concatenate([attended_early, attended_late], axis=1)]
    pallas_call x2 -> x3, Pallas kernels: 25.7 us -> 27 us  [the longest x2 26.1 us: attend(): pl.pallas_call(functools.partial(attention_kernel, slot_count, placed), o...]
  transfers between devices with their start and end apart: 5 -> 6, of which waited for: 4 -> 3; matrix products, arithmetic and copies ran while one was open for 8% -> 13% of each run, Pallas kernels for 1% -> 16%
where the time goes in v3:
time: 184 us; the launch traced here: 182 us
  blocking collectives  51.4 us (28%)
  Pallas kernels  29.7 us (16%)
  starting transfers between devices  26.6 us (14%)
  waiting for transfers between devices  26 us (14%)
  matrix products  17.3 us (9%)
  other arithmetic  15 us (8%)
  local copies, waits for them, and re-layouts  13.6 us (7%)
  between operations  2.61 us (1%)
    pallas_call x2, Pallas kernels, attend(): pl.pallas_call(functools.partial(attention_kernel, slot_count, placed), o...  26.1 us
    all_to_all x1, blocking collectives, shards(): lax.all_to_all(packed, 'dp', split_axis=0, concat_axis=0, tiled=True)  20.8 us
    all_gather x1, blocking collectives, shards(): lax.all_gather(part.astype(jnp.bfloat16), 'mp', axis=0, tiled=True)  17.9 us
    all_to_all x1, waiting for transfers between devices, shards(): lax.all_to_all(partial_mix.astype(jnp.bfloat16).reshape(planes, share, co...  14.7 us
    psum x1, blocking collectives, shards(): square_sum, signal = lax.psum((square_sum, signal), 'dp')  12.7 us
    unnamed x32, local copies, waits for them, and re-layouts  11.4 us
    all_to_all x2, starting transfers between devices, share_rows(): lax.all_to_all(copies, 'dp', split_axis=0, concat_axis=0, tiled=True)  8.39 us
    dot_general x1, matrix products, shards(): lax.dot_general(pooled_all, upstream_half, (((0,), (0,)), ((), ())), pref...  6.14 us
  transfers between devices with their start and end apart: 6, of which 3 were waited for; matrix products, arithmetic and copies ran while one was open for 13% of the time, Pallas kernels for 16%

profile of v3, /device:TPU:0, one launch (start us, length us, event | category | flops | bytes accessed | tf_op | source)
XLA Modules:
  0.0 182.2 jit_solution(18125250935272773442)
XLA Ops:
  6.7 20.8 %all_to_all.35 = bf16[8,6,8,1408]{3,2,1,0:T(8,128)(2,1)} all-to-all(bf16[8,6,8,1408]{3,2,1,0:T(8,128)(2,1)S(1)} %bitcast.21), channel_id=1, replica_groups=mesh['dp'=8,'mp'=4] {'dp'}, dimensions={0} | all-to-all | bytes 2162688 | tf_op jit(solution)/shard_map/all_to_all | solution.py:169
  27.5 4.2 %all-to-all-start.1 = ((bf16[8,6,8,768]{3,2,1,0:T(8,128)(2,1)}), bf16[8,6,8,768]{3,2,1,0:T(8,128)(2,1)}, u32[]{:S(2)}, u32[]{:S(2)}) async-start(bf16[8,6,8,768]{3,2,1,0:T(8,128)(2,1)} %bitcast.22), calls=%async_computation.1 | async-start | bytes 1179648 | tf_op jit(solution)/shard_map/all_to_all | solution.py:171
  33.0 1.9 %copy-done.3 = bf16[2,1,1024,768]{3,2,1,0:T(8,128)(2,1)S(1)} copy-done((bf16[2,1,1024,768]{3,2,1,0:T(8,128)(2,1)S(1)}, bf16[2,1,1024,768]{3,2,1,0:T(8,128)(2,1)}, u32[]{:S(2)}) %copy-start.3) | copy-done | bytes 3145752
  34.9 13.7 %attention_early.1 = (bf16[384,768]{1,0:T(8,128)(2,1)S(1)}, bf16[48,896]{1,0:T(8,128)(2,1)S(1)}) custom-call(s32[24]{0:T(128)S(1)} %pad_add_fusion.meta, bf16[384,1408]{1,0:T(8,128)(2,1)S(1)} %bitcast.14, bf16[384,1408]{1,0:T(8,128)(2,1)S(1)} %bitcast.15, bf16[384,1408]{1,0:T(8,128)(2,1)S(1)} %bitcast.16, bf16[384,1408]{1,0:T(8,128)(2,1)S(1)} %bitcast.17, ...), custom_call_target="tpu_custom_call" | custom-call | flops 1207959552 | bytes 2359296 | tf_op jit(solution)/shard_map/attention_early/pallas_call | solution.py:180
  50.4 4.2 %all-to-all-start.3 = ((bf16[8,48,896]{2,1,0:T(8,128)(2,1)}), bf16[8,48,896]{2,1,0:T(8,128)(2,1)}, u32[]{:S(2)}, u32[]{:S(2)}) async-start(bf16[8,48,896]{2,1,0:T(8,128)(2,1)} %broadcast_in_dim.10), calls=%async_computation.3 | async-start | bytes 1376256 | tf_op jit(solution)/shard_map/all_to_all | solution.py:222
  55.8 1.9 %copy-done.4 = bf16[2,1,1024,768]{3,2,1,0:T(8,128)(2,1)S(1)} copy-done((bf16[2,1,1024,768]{3,2,1,0:T(8,128)(2,1)S(1)}, bf16[2,1,1024,768]{3,2,1,0:T(8,128)(2,1)}, u32[]{:S(2)}) %copy-start.4) | copy-done | bytes 3145752
  57.7 12.4 %attention_late.1 = (bf16[384,768]{1,0:T(8,128)(2,1)S(1)}, bf16[48,768]{1,0:T(8,128)(2,1)S(1)}) custom-call(s32[24]{0:T(128)S(1)} %pad_add_fusion.meta, bf16[384,768]{1,0:T(8,128)(2,1)} %bitcast.4.query, bf16[384,1408]{1,0:T(8,128)(2,1)S(1)} %bitcast.18, bf16[384,1408]{1,0:T(8,128)(2,1)S(1)} %bitcast.19, bf16[384,1408]{1,0:T(8,128)(2,1)S(1)} %bitcast.20, ...), custom_call_target="tpu_custom_call" | custom-call | flops 1207959552 | bytes 2359296 | tf_op jit(solution)/shard_map/attention_late/pallas_call | solution.py:180
  71.8 4.2 %all-to-all-start.4 = ((bf16[8,48,768]{2,1,0:T(8,128)(2,1)}), bf16[8,48,768]{2,1,0:T(8,128)(2,1)}, u32[]{:S(2)}, u32[]{:S(2)}) async-start(bf16[8,48,768]{2,1,0:T(8,128)(2,1)} %broadcast_in_dim.12), calls=%async_computation.4 | async-start | bytes 1179648 | tf_op jit(solution)/shard_map/all_to_all | solution.py:222
  78.1 2.3 %convolution_convert_fusion.3 = bf16[384,768]{1,0:T(8,128)(2,1)} fusion(bf16[384,896]{1,0:T(8,128)(2,1)} %bitcast.7, s32[384]{0:T(512)S(1)} %add_select_fusion.2), kind=kOutput, calls=%fused_computation.15 | convolution fusion | flops 226934784 | bytes 1181184 | tf_op jit(solution)/shard_map/dot_general | solution.py:248
  80.5 5.9 %all-to-all-done.4 = bf16[8,48,768]{2,1,0:T(8,128)(2,1)} async-done(((bf16[8,48,768]{2,1,0:T(8,128)(2,1)}), bf16[8,48,768]{2,1,0:T(8,128)(2,1)}, u32[]{:S(2)}, u32[]{:S(2)}) %all-to-all-start.4) | async-done | bytes 589856 | tf_op jit(solution)/shard_map/all_to_all | solution.py:222
  88.0 3.5 %convolution_convert_fusion.1 = bf16[384,1024]{1,0:T(8,128)(2,1)} fusion(bf16[1536,1024]{1,0:T(8,128)(2,1)S(1)} %copy-done, bf16[384,768]{1,0:T(8,128)(2,1)S(1)} %convolution_convert_fusion.2, bf16[384,768]{1,0:T(8,128)(2,1)} %convolution_convert_fusion.3), kind=kOutput, calls=%fused_computation.13 | convolution fusion | flops 1210712064 | bytes 5111808 | tf_op jit(solution)/shard_map/dot_general | solution.py:254
  91.5 5.0 %all-to-all-start.5 = ((bf16[4,96,1024]{2,1,0:T(8,128)(2,1)}), bf16[4,96,1024]{2,1,0:T(8,128)(2,1)}, u32[]{:S(2)}, u32[]{:S(2)}) async-start(bf16[4,96,1024]{2,1,0:T(8,128)(2,1)} %bitcast.25), calls=%async_computation.5 | async-start | bytes 1572864 | tf_op jit(solution)/shard_map/all_to_all | solution.py:257
  97.0 2.3 %pad_maximum_fusion = bf16[384,1536]{1,0:T(8,128)(2,1)} fusion(bf16[384,768]{1,0:T(8,128)(2,1)} %copy-done.9, bf16[384,768]{1,0:T(8,128)(2,1)} %copy-done.8), kind=kLoop, calls=%fused_computation.16 | loop fusion | flops 2359296 | bytes 2359296 | tf_op jit(solution)/shard_map/concatenate | solution.py:229
  99.3 14.7 %all-to-all-done.5 = bf16[4,96,1024]{2,1,0:T(8,128)(2,1)} async-done(((bf16[4,96,1024]{2,1,0:T(8,128)(2,1)}), bf16[4,96,1024]{2,1,0:T(8,128)(2,1)}, u32[]{:S(2)}, u32[]{:S(2)}) %all-to-all-start.5) | async-done | bytes 786464 | tf_op jit(solution)/shard_map/all_to_all | solution.py:257
  114.0 4.8 %all-to-all-start.2 = ((bf16[8,6,8,1536]{3,2,1,0:T(8,128)(2,1)}), bf16[8,6,8,1536]{3,2,1,0:T(8,128)(2,1)}, u32[]{:S(2)}, u32[]{:S(2)}) async-start(bf16[8,6,8,1536]{3,2,1,0:T(8,128)(2,1)} %bitcast.23), calls=%async_computation.2 | async-start | bytes 2359296 | tf_op jit(solution)/shard_map/all_to_all | solution.py:231
  121.1 17.9 %all_gather.3 = bf16[384,1024]{1,0:T(8,128)(2,1)S(1)} all-gather(bf16[96,1024]{1,0:T(8,128)(2,1)S(1)} %add_convert_fusion), channel_id=1, replica_groups=mesh['dp'=8,'mp'=4] {'mp'}, dimensions={0}, use_global_device_ids=true | all-gather | bytes 983040 | tf_op jit(solution)/shard_map/all_gather | solution.py:267
  140.3 12.7 %all-reduce = (f32[384]{0:T(512)S(1)}, f32[384]{0:T(512)S(1)}) all-reduce(f32[384]{0:T(512)S(1)} %get-tuple-element.19, f32[384]{0:T(512)S(1)} %get-tuple-element.18), channel_id=1, replica_groups=mesh['dp'=8,'mp'=4] {'dp'}, use_global_device_ids=true, to_apply=%region_7.8 | all-reduce | flops 768 | bytes 6144 | tf_op jit(solution)/shard_map/psum | solution.py:272
  154.0 3.8 %convolution_convert_fusion = bf16[384,1536]{1,0:T(8,128)(2,1)} fusion(bf16[1536,1024]{1,0:T(8,128)(2,1)S(1)} %copy-done, bf16[384,1024]{1,0:T(8,128)(2,1)} %copy-done.10, f32[384]{0:T(512)S(1)} %get-tuple-element.25, f32[384]{0:T(512)S(1)} %get-tuple-element.24, f32[1024]{0:T(1024)S(1)} %mul.123), kind=kOutput, calls=%fused_computation | convolution fusion | flops 1210515456 | bytes 5118976 | tf_op jit(solution)/shard_map/dot_general | solution.py:281
  157.8 4.3 %all-to-all-start.6 = ((bf16[8,48,1536]{2,1,0:T(8,128)(2,1)}), bf16[8,48,1536]{2,1,0:T(8,128)(2,1)}, u32[]{:S(2)}, u32[]{:S(2)}) async-start(bf16[8,48,1536]{2,1,0:T(8,128)(2,1)} %bitcast.24), calls=%async_computation.6 | async-start | bytes 2359296 | tf_op jit(solution)/shard_map/all_to_all | solution.py:287
  162.0 2.6 %unpack.1 = bf16[48,8,1536]{2,1,0:T(8,128)(2,1)} custom-call(s32[48]{0:T(128)S(1)} %multiply_add_fusion.meta, bf16[48,8,1536]{2,1,0:T(8,128)(2,1)} %bitcast.6.returned), custom_call_target="tpu_custom_call" | custom-call | tf_op jit(solution)/shard_map/unpack/pallas_call | solution.py:232
  165.3 2.0 %fusion.5 = f32[1024]{0:T(1024)} fusion(bf16[384,1024]{1,0:T(8,128)(2,1)} %copy-done.10, f32[1024]{0:T(1024)S(1)} %copy-done.12, f32[384]{0:T(512)S(1)} %get-tuple-element.24), kind=kLoop, calls=%fused_computation.11 | loop fusion | flops 1571840 | bytes 796160 | tf_op jit(solution)/shard_map/reduce_sum | solution.py:279
  167.3 6.1 %fusion.6 = f32[1536,1024]{1,0:T(8,128)} fusion(bf16[384,768]{1,0:T(8,128)(2,1)} %copy-done.11, bf16[384,768]{1,0:T(8,128)(2,1)} %convolution_convert_fusion.3, bf16[384,1024]{1,0:T(8,128)(2,1)} %copy-done.10, f32[384]{0:T(512)S(1)} %get-tuple-element.25, f32[384]{0:T(512)S(1)} %get-tuple-element.24, f32[1024]{0:T(1024)S(1)} %mul.123), kind=kOutput, calls=%fused_computation.18 | convolution fusion | flops 1212284928 | bytes 8264704 | tf_op jit(solution)/shard_map/dot_general | solution.py:294
  173.5 5.4 %all-to-all-done.6 = bf16[8,48,1536]{2,1,0:T(8,128)(2,1)} async-done(((bf16[8,48,1536]{2,1,0:T(8,128)(2,1)}), bf16[8,48,1536]{2,1,0:T(8,128)(2,1)}, u32[]{:S(2)}, u32[]{:S(2)}) %all-to-all-start.6) | async-done | bytes 1179680 | tf_op jit(solution)/shard_map/all_to_all | solution.py:287
  178.9 2.2 %convert_reduce_fusion = f32[48,1536]{1,0:T(8,128)} fusion(bf16[8,48,1536]{2,1,0:T(8,128)(2,1)} %all-to-all-done.6), kind=kLoop, calls=%fused_computation.5 | loop fusion | flops 1105920 | bytes 1474560 | tf_op jit(solution)/shard_map/reduce_sum | solution.py:297
  (57 shorter events, 20.7 us)
Async XLA Ops:
  0.6 87.3 %copy-start = (bf16[1536,1024]{1,0:T(8,128)(2,1)S(1)}, bf16[1536,1024]{1,0:T(8,128)(2,1)}, u32[]{:S(2)}) copy-start(bf16[1536,1024]{1,0:T(8,128)(2,1)} %param.17) | copy-start | bytes 9437188
  3.2 1.3 copy-start.5
  4.5 1.3 copy-start.6
  6.7 20.8 %copy-start.7 = (bf16[48,8,768]{2,1,0:T(8,128)(2,1)}, bf16[48,8,768]{2,1,0:T(8,128)(2,1)S(1)}, u32[]{:S(2)}) copy-start(bf16[48,8,768]{2,1,0:T(8,128)(2,1)S(1)} %get-tuple-element.14) | copy-start | bytes 1769476
  27.5 22.0 %all-to-all-start.1 = ((bf16[8,6,8,768]{3,2,1,0:T(8,128)(2,1)}), bf16[8,6,8,768]{3,2,1,0:T(8,128)(2,1)}, u32[]{:S(2)}, u32[]{:S(2)}) async-start(bf16[8,6,8,768]{3,2,1,0:T(8,128)(2,1)} %bitcast.22), calls=%async_computation.1 | async-start | bytes 1179648 | tf_op jit(solution)/shard_map/all_to_all | solution.py:171
  31.8 1.2 copy-start.1
  33.0 1.9 %copy-start.3 = (bf16[2,1,1024,768]{3,2,1,0:T(8,128)(2,1)S(1)}, bf16[2,1,1024,768]{3,2,1,0:T(8,128)(2,1)}, u32[]{:S(2)}) copy-start(bf16[2,1,1024,768]{3,2,1,0:T(8,128)(2,1)} %cache.3) | copy-start | bytes 9437188
  48.6 0.8 copy-start.8
  50.4 20.5 %all-to-all-start.3 = ((bf16[8,48,896]{2,1,0:T(8,128)(2,1)}), bf16[8,48,896]{2,1,0:T(8,128)(2,1)}, u32[]{:S(2)}, u32[]{:S(2)}) async-start(bf16[8,48,896]{2,1,0:T(8,128)(2,1)} %broadcast_in_dim.10), calls=%async_computation.3 | async-start | bytes 1376256 | tf_op jit(solution)/shard_map/all_to_all | solution.py:222
  54.6 1.2 copy-start.2
  55.8 1.9 %copy-start.4 = (bf16[2,1,1024,768]{3,2,1,0:T(8,128)(2,1)S(1)}, bf16[2,1,1024,768]{3,2,1,0:T(8,128)(2,1)}, u32[]{:S(2)}) copy-start(bf16[2,1,1024,768]{3,2,1,0:T(8,128)(2,1)} %cache.3) | copy-start | bytes 9437188
  70.1 0.8 copy-start.9
  71.8 14.7 %all-to-all-start.4 = ((bf16[8,48,768]{2,1,0:T(8,128)(2,1)}), bf16[8,48,768]{2,1,0:T(8,128)(2,1)}, u32[]{:S(2)}, u32[]{:S(2)}) async-start(bf16[8,48,768]{2,1,0:T(8,128)(2,1)} %broadcast_in_dim.12), calls=%async_computation.4 | async-start | bytes 1179648 | tf_op jit(solution)/shard_map/all_to_all | solution.py:222
  88.0 3.6 %copy-start.11 = (bf16[384,768]{1,0:T(8,128)(2,1)}, bf16[384,768]{1,0:T(8,128)(2,1)S(1)}, u32[]{:S(2)}) copy-start(bf16[384,768]{1,0:T(8,128)(2,1)S(1)} %convolution_convert_fusion.2) | copy-start | bytes 1769476
  91.5 5.0 %copy-start.15 = (s32[384]{0:T(512)S(1)}, s32[384]{0:T(512)}, u32[]{:S(2)}) copy-start(s32[384]{0:T(512)} %param.15) | copy-start | bytes 4612
  91.5 5.5 %copy-start.12 = (f32[1024]{0:T(1024)S(1)}, f32[1024]{0:T(1024)}, u32[]{:S(2)}) copy-start(f32[1024]{0:T(1024)} %param.18) | copy-start | bytes 12292
  91.5 5.5 %copy-start.14 = (f32[1024]{0:T(1024)S(1)}, f32[1024]{0:T(1024)}, u32[]{:S(2)}) copy-start(f32[1024]{0:T(1024)} %param.19) | copy-start | bytes 12292
  91.5 22.5 %all-to-all-start.5 = ((bf16[4,96,1024]{2,1,0:T(8,128)(2,1)}), bf16[4,96,1024]{2,1,0:T(8,128)(2,1)}, u32[]{:S(2)}, u32[]{:S(2)}) async-start(bf16[4,96,1024]{2,1,0:T(8,128)(2,1)} %bitcast.25), calls=%async_computation.5 | async-start | bytes 1572864 | tf_op jit(solution)/shard_map/all_to_all | solution.py:257
  114.0 43.7 %all-to-all-start.2 = ((bf16[8,6,8,1536]{3,2,1,0:T(8,128)(2,1)}), bf16[8,6,8,1536]{3,2,1,0:T(8,128)(2,1)}, u32[]{:S(2)}, u32[]{:S(2)}) async-start(bf16[8,6,8,1536]{3,2,1,0:T(8,128)(2,1)} %bitcast.23), calls=%async_computation.2 | async-start | bytes 2359296 | tf_op jit(solution)/shard_map/all_to_all | solution.py:231
  139.0 0.9 copy-start.10
  153.0 4.8 %copy-start.13 = (f32[384]{0:T(512)}, f32[384]{0:T(512)S(1)}, u32[]{:S(2)}) copy-start(f32[384]{0:T(512)S(1)} %fusion.19) | copy-start | bytes 4612
  157.8 21.1 %all-to-all-start.6 = ((bf16[8,48,1536]{2,1,0:T(8,128)(2,1)}), bf16[8,48,1536]{2,1,0:T(8,128)(2,1)}, u32[]{:S(2)}, u32[]{:S(2)}) async-start(bf16[8,48,1536]{2,1,0:T(8,128)(2,1)} %bitcast.24), calls=%async_computation.6 | async-start | bytes 2359296 | tf_op jit(solution)/shard_map/all_to_all | solution.py:287

commit v4 on v3

--- a/solution.py
+++ b/solution.py
@@ -53,11 +53,9 @@
     lax.fori_loop(0, slots, body, 0)
 
 
-def attention_kernel(slot_count, placed, meta, query, own_k, own_v, lens, cache, out, pooled):
+def attention_kernel(slot_count, meta, query, own_k, own_v, lens, cache, out):
     rows = query.shape[0]
-    head = pl.program_id(0)
     chunk = 128
-    blocks = chunk // slot_count
     scale = math.log2(math.e) / math.sqrt(HD)
     contract = (((1,), (1,)), ((), ()))
     row = lax.broadcasted_iota(jnp.int32, (chunk, chunk), 0)
@@ -67,9 +65,6 @@
     causal = (row // slot_count == col // slot_count) & (s <= t)
     s_float = s.astype(jnp.float32)
     t_float = t.astype(jnp.float32)
-    gather = lax.broadcasted_iota(jnp.int32, (blocks, chunk), 0)
-    member = lax.broadcasted_iota(jnp.int32, (blocks, chunk), 1)
-    gather = jnp.where(gather == member // slot_count, 1.0, 0.0).astype(jnp.bfloat16)
     for start in range(0, rows, chunk):
         here = pl.ds(start, chunk)
         q = query[here, :]
@@ -89,19 +84,6 @@
         )
         value = jnp.where(t_float < length, value / total, 0.0)
         out[here, :] = value.astype(jnp.bfloat16)
-        last = jnp.where(t_float == length - 1.0, value, 0.0)
-        last = jnp.dot(gather, last.astype(jnp.bfloat16), preferred_element_type=jnp.float32)
-        there = pl.ds(start // slot_count, blocks)
-        pooled[there, pl.ds(pl.multiple_of(head * HD, HD), HD)] = last.astype(jnp.bfloat16)
-
-        if placed:
-
-            @pl.when(head == 0)
-            def _():
-                place = lens[here, :].astype(jnp.float32).reshape(blocks, slot_count, HD)
-                pooled[there, pl.ds(pooled.shape[1] - HD, HD)] = jnp.max(place, axis=1).astype(
-                    jnp.bfloat16
-                )
 
 
 def unpack_kernel(meta, returned, out):
@@ -174,15 +156,11 @@
     arrived = arrived.reshape(rows, packed_width)
     block = (rows, HD)
 
-    def attend(query, head_base, heads, placed):
-        pooled_width = (heads + placed) * HD
+    def attend(query, head_base, heads):
         at = lambda meta, h: meta[local_heads + head_base + h]
         return pl.pallas_call(
-            functools.partial(attention_kernel, slot_count, placed),
-            out_shape=(
-                jax.ShapeDtypeStruct((rows, heads * HD), jnp.bfloat16),
-                jax.ShapeDtypeStruct((capacity, pooled_width), jnp.bfloat16),
-            ),
+            functools.partial(attention_kernel, slot_count),
+            out_shape=jax.ShapeDtypeStruct((rows, heads * HD), jnp.bfloat16),
             grid_spec=pltpu.PrefetchScalarGridSpec(
                 num_scalar_prefetch=1,
                 grid=(heads,),
@@ -196,10 +174,7 @@
                         lambda h, meta: (0, 0, 0, meta[head_base + h]),
                     ),
                 ],
-                out_specs=(
-                    pl.BlockSpec(block, lambda h, meta: (0, h)),
-                    pl.BlockSpec((capacity, pooled_width), lambda h, meta: (0, 0)),
-                ),
+                out_specs=pl.BlockSpec(block, lambda h, meta: (0, h)),
             ),
             compiler_params=params,
             cost_estimate=pl.CostEstimate(
@@ -207,7 +182,7 @@
                 bytes_accessed=8 * rows * heads * HD,
                 transcendentals=rows * heads * prompt_cache.shape[2],
             ),
-            name="attention_early" if placed else "attention_late",
+            name="attention_late" if head_base else "attention_early",
         )(
             jnp.concatenate([head_kv, head_kv - first_head]).astype(jnp.int32),
             query,
@@ -222,9 +197,18 @@
         copies = lax.all_to_all(copies, "dp", split_axis=0, concat_axis=0, tiled=True)
         return copies.reshape(groups * own.shape[0], own.shape[1])
 
-    attended_early, pooled_early = attend(arrived, 0, early, True)
+    tags = arrived.reshape(capacity, slot_count, packed_width)[:, 0, packed_width - HD :]
+    last_row = tags[:, :1].astype(jnp.int32) - 1 == jnp.arange(slot_count)[None, :]
+
+    def last_rows(attended):
+        by_block = attended.reshape(capacity, slot_count, attended.shape[1]).astype(jnp.float32)
+        return jnp.sum(jnp.where(last_row[:, :, None], by_block, 0.0), axis=1).astype(jnp.bfloat16)
+
+    attended_early = attend(arrived, 0, early)
+    pooled_early = jnp.concatenate([last_rows(attended_early), tags], axis=1)
     pooled_slots = share_rows(pooled_early)
-    attended_late, pooled_late = attend(late, early, local_heads - early, False)
+    attended_late = attend(late, early, local_heads - early)
+    pooled_late = last_rows(attended_late)
     pooled_late = share_rows(pooled_late)
     attended = jnp.concatenate([attended_early, attended_late], axis=1)
     result = attended.reshape(groups, per_owner, slot_count, head_width)

time: 184 us -> 187 us (1.016)
  blocking collectives: 51.4 us -> 66.9 us
  Pallas kernels: 29.7 us -> 22.6 us
  starting transfers between devices: 26.6 us -> 22.4 us
    all_to_all x0 -> x1, blocking collectives: none -> 15.5 us  [share_rows(): lax.all_to_all(copies, 'dp', split_axis=0, concat_axis=0, tiled=True)]
    pallas_call x2, Pallas kernels: 26.1 us -> 19.1 us  [attend(): pl.pallas_call(functools.partial(attention_kernel, slot_count), out_shape...]
    all_to_all x2 -> x1, starting transfers between devices: 8.39 us -> 4.19 us  [share_rows(): lax.all_to_all(copies, 'dp', split_axis=0, concat_axis=0, tiled=True)]
    unnamed x32 -> x35, local copies, waits for them, and re-layouts: 11.4 us -> 10.6 us
    all_to_all x2 -> x1, waiting for transfers between devices: 5.93 us -> 5.93 us  [share_rows(): lax.all_to_all(copies, 'dp', split_axis=0, concat_axis=0, tiled=True)]
  transfers between devices with their start and end apart: 6 -> 5, of which waited for: 3 -> 3; matrix products, arithmetic and copies ran while one was open for 13% -> 12% of each run, Pallas kernels for 16% -> 6%
where the time goes in v4:
time: 187 us; the launch traced here: 186 us
  blocking collectives  66.9 us (36%)
  waiting for transfers between devices  26 us (14%)
  Pallas kernels  22.6 us (12%)
  starting transfers between devices  22.4 us (12%)
  matrix products  17.3 us (9%)
  other arithmetic  16.2 us (9%)
  local copies, waits for them, and re-layouts  11.9 us (6%)
  between operations  2.65 us (1%)
    all_to_all x1, blocking collectives, shards(): lax.all_to_all(packed, 'dp', split_axis=0, concat_axis=0, tiled=True)  20.8 us
    pallas_call x2, Pallas kernels, attend(): pl.pallas_call(functools.partial(attention_kernel, slot_count), out_shape...  19.1 us
    all_gather x1, blocking collectives, shards(): lax.all_gather(part.astype(jnp.bfloat16), 'mp', axis=0, tiled=True)  17.9 us
    all_to_all x1, blocking collectives, share_rows(): lax.all_to_all(copies, 'dp', split_axis=0, concat_axis=0, tiled=True)  15.5 us
    all_to_all x1, waiting for transfers between devices, shards(): lax.all_to_all(partial_mix.astype(jnp.bfloat16).reshape(planes, share, co...  14.7 us
    psum x1, blocking collectives, shards(): square_sum, signal = lax.psum((square_sum, signal), 'dp')  12.7 us
    unnamed x35, local copies, waits for them, and re-layouts  10.6 us
    dot_general x1, matrix products, shards(): lax.dot_general(pooled_all, upstream_half, (((0,), (0,)), ((), ())), pref...  6.14 us
  transfers between devices with their start and end apart: 5, of which 3 were waited for; matrix products, arithmetic and copies ran while one was open for 12% of the time, Pallas kernels for 6%

profile of v4, /device:TPU:0, one launch (start us, length us, event | category | flops | bytes accessed | tf_op | source)
XLA Modules:
  0.0 186.1 jit_solution(10900862089184650669)
XLA Ops:
  6.7 20.8 %all_to_all.35 = bf16[8,6,8,1408]{3,2,1,0:T(8,128)(2,1)} all-to-all(bf16[8,6,8,1408]{3,2,1,0:T(8,128)(2,1)S(1)} %bitcast.32), channel_id=1, replica_groups=mesh['dp'=8,'mp'=4] {'dp'}, dimensions={0} | all-to-all | bytes 2162688 | tf_op jit(solution)/shard_map/all_to_all | solution.py:151
  27.5 4.2 %all-to-all-start.1 = ((bf16[8,6,8,768]{3,2,1,0:T(8,128)(2,1)}), bf16[8,6,8,768]{3,2,1,0:T(8,128)(2,1)}, u32[]{:S(2)}, u32[]{:S(2)}) async-start(bf16[8,6,8,768]{3,2,1,0:T(8,128)(2,1)} %bitcast.33), calls=%async_computation.1 | async-start | bytes 1179648 | tf_op jit(solution)/shard_map/all_to_all | solution.py:153
  33.0 1.9 %copy-done.3 = bf16[2,1,1024,768]{3,2,1,0:T(8,128)(2,1)S(1)} copy-done((bf16[2,1,1024,768]{3,2,1,0:T(8,128)(2,1)S(1)}, bf16[2,1,1024,768]{3,2,1,0:T(8,128)(2,1)}, u32[]{:S(2)}) %copy-start.3) | copy-done | bytes 3145752
  34.9 9.1 %attention_early.1 = bf16[384,768]{1,0:T(8,128)(2,1)S(1)} custom-call(s32[24]{0:T(128)S(1)} %pad_add_fusion.meta, bf16[384,1408]{1,0:T(8,128)(2,1)S(1)} %bitcast.24, bf16[384,1408]{1,0:T(8,128)(2,1)S(1)} %bitcast.25, bf16[384,1408]{1,0:T(8,128)(2,1)S(1)} %bitcast.26, bf16[384,1408]{1,0:T(8,128)(2,1)S(1)} %bitcast.27, bf16[2,1,1024,768]{3,2,1,0:T(8,128)(2,1)S(1)} %copy-done.3), custom_call_target="tpu_custom_call" | custom-call | flops 1207959552 | bytes 2359296 | tf_op jit(solution)/shard_map/attention_early/pallas_call | solution.py:161
  46.1 1.9 %copy-done.4 = bf16[2,1,1024,768]{3,2,1,0:T(8,128)(2,1)S(1)} copy-done((bf16[2,1,1024,768]{3,2,1,0:T(8,128)(2,1)S(1)}, bf16[2,1,1024,768]{3,2,1,0:T(8,128)(2,1)}, u32[]{:S(2)}) %copy-start.4) | copy-done | bytes 3145752
  48.0 9.9 %attention_late.1 = bf16[384,768]{1,0:T(8,128)(2,1)S(1)} custom-call(s32[24]{0:T(128)S(1)} %pad_add_fusion.meta, bf16[384,768]{1,0:T(8,128)(2,1)} %bitcast.4.query, bf16[384,1408]{1,0:T(8,128)(2,1)S(1)} %bitcast.28, bf16[384,1408]{1,0:T(8,128)(2,1)S(1)} %bitcast.29, bf16[384,1408]{1,0:T(8,128)(2,1)S(1)} %bitcast.30, bf16[2,1,1024,768]{3,2,1,0:T(8,128)(2,1)S(1)} %copy-done.4), custom_call_target="tpu_custom_call" | custom-call | flops 1207959552 | bytes 2359296 | tf_op jit(solution)/shard_map/attention_late/pallas_call | solution.py:161
  59.3 15.5 %all_to_all.36 = bf16[8,48,896]{2,1,0:T(8,128)(2,1)} all-to-all(bf16[8,48,896]{2,1,0:T(8,128)(2,1)S(1)} %broadcast_in_dim.28), channel_id=1, replica_groups=mesh['dp'=8,'mp'=4] {'dp'}, dimensions={0} | all-to-all | bytes 1376256 | tf_op jit(solution)/shard_map/all_to_all | solution.py:197
  75.7 4.2 %all-to-all-start.4 = ((bf16[8,48,768]{2,1,0:T(8,128)(2,1)}), bf16[8,48,768]{2,1,0:T(8,128)(2,1)}, u32[]{:S(2)}, u32[]{:S(2)}) async-start(bf16[8,48,768]{2,1,0:T(8,128)(2,1)} %broadcast_in_dim.31), calls=%async_computation.4 | async-start | bytes 1179648 | tf_op jit(solution)/shard_map/all_to_all | solution.py:197
  82.1 2.3 %convolution_convert_fusion.3 = bf16[384,768]{1,0:T(8,128)(2,1)} fusion(bf16[384,896]{1,0:T(8,128)(2,1)} %bitcast.38, s32[384]{0:T(512)S(1)} %add_select_fusion.2), kind=kOutput, calls=%fused_computation.15 | convolution fusion | flops 226934784 | bytes 1181184 | tf_op jit(solution)/shard_map/dot_general | solution.py:232
  84.4 5.9 %all-to-all-done.4 = bf16[8,48,768]{2,1,0:T(8,128)(2,1)} async-done(((bf16[8,48,768]{2,1,0:T(8,128)(2,1)}), bf16[8,48,768]{2,1,0:T(8,128)(2,1)}, u32[]{:S(2)}, u32[]{:S(2)}) %all-to-all-start.4) | async-done | bytes 589856 | tf_op jit(solution)/shard_map/all_to_all | solution.py:197
  91.9 3.5 %convolution_convert_fusion.1 = bf16[384,1024]{1,0:T(8,128)(2,1)} fusion(bf16[1536,1024]{1,0:T(8,128)(2,1)S(1)} %copy-done, bf16[384,768]{1,0:T(8,128)(2,1)S(1)} %convolution_convert_fusion.2, bf16[384,768]{1,0:T(8,128)(2,1)} %convolution_convert_fusion.3), kind=kOutput, calls=%fused_computation.13 | convolution fusion | flops 1210712064 | bytes 5111808 | tf_op jit(solution)/shard_map/dot_general | solution.py:238
  95.4 5.0 %all-to-all-start.5 = ((bf16[4,96,1024]{2,1,0:T(8,128)(2,1)}), bf16[4,96,1024]{2,1,0:T(8,128)(2,1)}, u32[]{:S(2)}, u32[]{:S(2)}) async-start(bf16[4,96,1024]{2,1,0:T(8,128)(2,1)} %bitcast.39), calls=%async_computation.5 | async-start | bytes 1572864 | tf_op jit(solution)/shard_map/all_to_all | solution.py:241
  100.9 2.3 %pad_maximum_fusion = bf16[384,1536]{1,0:T(8,128)(2,1)} fusion(bf16[384,768]{1,0:T(8,128)(2,1)} %copy-done.7, bf16[384,768]{1,0:T(8,128)(2,1)} %copy-done.5), kind=kLoop, calls=%fused_computation.16 | loop fusion | flops 2359296 | bytes 2359296 | tf_op jit(solution)/shard_map/concatenate | solution.py:213
  103.3 14.7 %all-to-all-done.5 = bf16[4,96,1024]{2,1,0:T(8,128)(2,1)} async-done(((bf16[4,96,1024]{2,1,0:T(8,128)(2,1)}), bf16[4,96,1024]{2,1,0:T(8,128)(2,1)}, u32[]{:S(2)}, u32[]{:S(2)}) %all-to-all-start.5) | async-done | bytes 786464 | tf_op jit(solution)/shard_map/all_to_all | solution.py:241
  118.0 4.8 %all-to-all-start.2 = ((bf16[8,6,8,1536]{3,2,1,0:T(8,128)(2,1)}), bf16[8,6,8,1536]{3,2,1,0:T(8,128)(2,1)}, u32[]{:S(2)}, u32[]{:S(2)}) async-start(bf16[8,6,8,1536]{3,2,1,0:T(8,128)(2,1)} %bitcast.34), calls=%async_computation.2 | async-start | bytes 2359296 | tf_op jit(solution)/shard_map/all_to_all | solution.py:215
  125.0 17.9 %all_gather.3 = bf16[384,1024]{1,0:T(8,128)(2,1)S(1)} all-gather(bf16[96,1024]{1,0:T(8,128)(2,1)S(1)} %add_convert_fusion), channel_id=1, replica_groups=mesh['dp'=8,'mp'=4] {'mp'}, dimensions={0}, use_global_device_ids=true | all-gather | bytes 983040 | tf_op jit(solution)/shard_map/all_gather | solution.py:251
  144.2 12.7 %all-reduce = (f32[384]{0:T(512)S(1)}, f32[384]{0:T(512)S(1)}) all-reduce(f32[384]{0:T(512)S(1)} %get-tuple-element.11, f32[384]{0:T(512)S(1)} %get-tuple-element.10), channel_id=1, replica_groups=mesh['dp'=8,'mp'=4] {'dp'}, use_global_device_ids=true, to_apply=%region_9.10 | all-reduce | flops 768 | bytes 6144 | tf_op jit(solution)/shard_map/psum | solution.py:256
  157.9 3.8 %convolution_convert_fusion = bf16[384,1536]{1,0:T(8,128)(2,1)} fusion(bf16[1536,1024]{1,0:T(8,128)(2,1)S(1)} %copy-done, bf16[384,1024]{1,0:T(8,128)(2,1)} %copy-done.11, f32[384]{0:T(512)S(1)} %get-tuple-element.19, f32[384]{0:T(512)S(1)} %get-tuple-element.18, f32[1024]{0:T(1024)S(1)} %mul.123), kind=kOutput, calls=%fused_computation | convolution fusion | flops 1210515456 | bytes 5118976 | tf_op jit(solution)/shard_map/dot_general | solution.py:265
  161.7 4.3 %all-to-all-start.6 = ((bf16[8,48,1536]{2,1,0:T(8,128)(2,1)}), bf16[8,48,1536]{2,1,0:T(8,128)(2,1)}, u32[]{:S(2)}, u32[]{:S(2)}) async-start(bf16[8,48,1536]{2,1,0:T(8,128)(2,1)} %bitcast.35), calls=%async_computation.6 | async-start | bytes 2359296 | tf_op jit(solution)/shard_map/all_to_all | solution.py:271
  165.9 2.6 %unpack.1 = bf16[48,8,1536]{2,1,0:T(8,128)(2,1)} custom-call(s32[48]{0:T(128)S(1)} %multiply_add_fusion.meta, bf16[48,8,1536]{2,1,0:T(8,128)(2,1)} %bitcast.6.returned), custom_call_target="tpu_custom_call" | custom-call | tf_op jit(solution)/shard_map/unpack/pallas_call | solution.py:216
  169.2 2.0 %fusion.5 = f32[1024]{0:T(1024)} fusion(bf16[384,1024]{1,0:T(8,128)(2,1)} %copy-done.11, f32[1024]{0:T(1024)S(1)} %copy-done.13, f32[384]{0:T(512)S(1)} %get-tuple-element.18), kind=kLoop, calls=%fused_computation.11 | loop fusion | flops 1571840 | bytes 796160 | tf_op jit(solution)/shard_map/reduce_sum | solution.py:263
  171.3 6.1 %fusion.8 = f32[1536,1024]{1,0:T(8,128)} fusion(bf16[384,768]{1,0:T(8,128)(2,1)} %copy-done.12, bf16[384,768]{1,0:T(8,128)(2,1)} %convolution_convert_fusion.3, bf16[384,1024]{1,0:T(8,128)(2,1)} %copy-done.11, f32[384]{0:T(512)S(1)} %get-tuple-element.19, f32[384]{0:T(512)S(1)} %get-tuple-element.18, f32[1024]{0:T(1024)S(1)} %mul.123), kind=kOutput, calls=%fused_computation.22 | convolution fusion | flops 1212284928 | bytes 8264704 | tf_op jit(solution)/shard_map/dot_general | solution.py:278
  177.4 5.4 %all-to-all-done.6 = bf16[8,48,1536]{2,1,0:T(8,128)(2,1)} async-done(((bf16[8,48,1536]{2,1,0:T(8,128)(2,1)}), bf16[8,48,1536]{2,1,0:T(8,128)(2,1)}, u32[]{:S(2)}, u32[]{:S(2)}) %all-to-all-start.6) | async-done | bytes 1179680 | tf_op jit(solution)/shard_map/all_to_all | solution.py:271
  182.8 2.2 %convert_reduce_fusion = f32[48,1536]{1,0:T(8,128)} fusion(bf16[8,48,1536]{2,1,0:T(8,128)(2,1)} %all-to-all-done.6), kind=kLoop, calls=%fused_computation.5 | loop fusion | flops 1105920 | bytes 1474560 | tf_op jit(solution)/shard_map/reduce_sum | solution.py:281
  (64 shorter events, 20.3 us)
Async XLA Ops:
  0.6 91.2 %copy-start = (bf16[1536,1024]{1,0:T(8,128)(2,1)S(1)}, bf16[1536,1024]{1,0:T(8,128)(2,1)}, u32[]{:S(2)}) copy-start(bf16[1536,1024]{1,0:T(8,128)(2,1)} %param.17) | copy-start | bytes 9437188
  3.2 1.3 copy-start.8
  4.5 1.3 copy-start.9
  6.7 20.8 %copy-start.10 = (bf16[48,8,768]{2,1,0:T(8,128)(2,1)}, bf16[48,8,768]{2,1,0:T(8,128)(2,1)S(1)}, u32[]{:S(2)}) copy-start(bf16[48,8,768]{2,1,0:T(8,128)(2,1)S(1)} %get-tuple-element.9) | copy-start | bytes 1769476
  27.5 17.4 %all-to-all-start.1 = ((bf16[8,6,8,768]{3,2,1,0:T(8,128)(2,1)}), bf16[8,6,8,768]{3,2,1,0:T(8,128)(2,1)}, u32[]{:S(2)}, u32[]{:S(2)}) async-start(bf16[8,6,8,768]{3,2,1,0:T(8,128)(2,1)} %bitcast.33), calls=%async_computation.1 | async-start | bytes 1179648 | tf_op jit(solution)/shard_map/all_to_all | solution.py:153
  31.8 1.2 copy-start.1
  33.0 1.9 %copy-start.3 = (bf16[2,1,1024,768]{3,2,1,0:T(8,128)(2,1)S(1)}, bf16[2,1,1024,768]{3,2,1,0:T(8,128)(2,1)}, u32[]{:S(2)}) copy-start(bf16[2,1,1024,768]{3,2,1,0:T(8,128)(2,1)} %cache.3) | copy-start | bytes 9437188
  44.1 0.8 copy-start.5
  44.9 1.2 copy-start.2
  46.1 1.9 %copy-start.4 = (bf16[2,1,1024,768]{3,2,1,0:T(8,128)(2,1)S(1)}, bf16[2,1,1024,768]{3,2,1,0:T(8,128)(2,1)}, u32[]{:S(2)}) copy-start(bf16[2,1,1024,768]{3,2,1,0:T(8,128)(2,1)} %cache.3) | copy-start | bytes 9437188
  48.0 10.2 %copy-start.6 = (bf16[384,768]{1,0:T(8,128)(2,1)S(1)}, bf16[384,768]{1,0:T(8,128)(2,1)}, u32[]{:S(2)}) copy-start(bf16[384,768]{1,0:T(8,128)(2,1)} %copy-done.5) | copy-start | bytes 1769476
  57.9 16.9 %copy-start.7 = (bf16[384,768]{1,0:T(8,128)(2,1)}, bf16[384,768]{1,0:T(8,128)(2,1)S(1)}, u32[]{:S(2)}) copy-start(bf16[384,768]{1,0:T(8,128)(2,1)S(1)} %attention_late.1) | copy-start | bytes 1769476
  75.7 14.7 %all-to-all-start.4 = ((bf16[8,48,768]{2,1,0:T(8,128)(2,1)}), bf16[8,48,768]{2,1,0:T(8,128)(2,1)}, u32[]{:S(2)}, u32[]{:S(2)}) async-start(bf16[8,48,768]{2,1,0:T(8,128)(2,1)} %broadcast_in_dim.31), calls=%async_computation.4 | async-start | bytes 1179648 | tf_op jit(solution)/shard_map/all_to_all | solution.py:197
  91.9 3.6 %copy-start.12 = (bf16[384,768]{1,0:T(8,128)(2,1)}, bf16[384,768]{1,0:T(8,128)(2,1)S(1)}, u32[]{:S(2)}) copy-start(bf16[384,768]{1,0:T(8,128)(2,1)S(1)} %convolution_convert_fusion.2) | copy-start | bytes 1769476
  95.4 5.0 %copy-start.16 = (s32[384]{0:T(512)S(1)}, s32[384]{0:T(512)}, u32[]{:S(2)}) copy-start(s32[384]{0:T(512)} %param.15) | copy-start | bytes 4612
  95.4 5.5 %copy-start.13 = (f32[1024]{0:T(1024)S(1)}, f32[1024]{0:T(1024)}, u32[]{:S(2)}) copy-start(f32[1024]{0:T(1024)} %param.18) | copy-start | bytes 12292
  95.4 5.5 %copy-start.15 = (f32[1024]{0:T(1024)S(1)}, f32[1024]{0:T(1024)}, u32[]{:S(2)}) copy-start(f32[1024]{0:T(1024)} %param.19) | copy-start | bytes 12292
  95.4 22.5 %all-to-all-start.5 = ((bf16[4,96,1024]{2,1,0:T(8,128)(2,1)}), bf16[4,96,1024]{2,1,0:T(8,128)(2,1)}, u32[]{:S(2)}, u32[]{:S(2)}) async-start(bf16[4,96,1024]{2,1,0:T(8,128)(2,1)} %bitcast.39), calls=%async_computation.5 | async-start | bytes 1572864 | tf_op jit(solution)/shard_map/all_to_all | solution.py:241
  118.0 43.7 %all-to-all-start.2 = ((bf16[8,6,8,1536]{3,2,1,0:T(8,128)(2,1)}), bf16[8,6,8,1536]{3,2,1,0:T(8,128)(2,1)}, u32[]{:S(2)}, u32[]{:S(2)}) async-start(bf16[8,6,8,1536]{3,2,1,0:T(8,128)(2,1)} %bitcast.34), calls=%async_computation.2 | async-start | bytes 2359296 | tf_op jit(solution)/shard_map/all_to_all | solution.py:215
  142.9 0.9 copy-start.11
  156.9 4.8 %copy-start.14 = (f32[384]{0:T(512)}, f32[384]{0:T(512)S(1)}, u32[]{:S(2)}) copy-start(f32[384]{0:T(512)S(1)} %fusion.21) | copy-start | bytes 4612
  161.7 21.1 %all-to-all-start.6 = ((bf16[8,48,1536]{2,1,0:T(8,128)(2,1)}), bf16[8,48,1536]{2,1,0:T(8,128)(2,1)}, u32[]{:S(2)}, u32[]{:S(2)}) async-start(bf16[8,48,1536]{2,1,0:T(8,128)(2,1)} %bitcast.35), calls=%async_computation.6 | async-start | bytes 2359296 | tf_op jit(solution)/shard_map/all_to_all | solution.py:271
